TPU v7x, 32 devices: a whole 2x2x4 slice. The times are simulated.
32 devices in a mesh: dp: 8 (over z, x), fsdp: 4 (over y, core).
Axes of the slice: x: 2, y: 2, z: 4, core: 2. Of those that a mesh axis runs over, the one named last changes fastest.
Arguments:
- tokens: bfloat16 [16, 256, 1024], P('dp', 'fsdp'), may hold values from -6 to 6
- masks: int32 [16, 256], P('dp', 'fsdp'), may hold values from 0 to 1, as said below
- cotangent: bfloat16 [16, 256, 1024], P('dp', 'fsdp')
- w_in: float32 [1024, 10, 1024], P('dp', None, 'fsdp'), may hold values from -0.09375 to 0.09375
- w_out: float32 [6, 1024, 1024], P(None, 'fsdp', 'dp')
- vectors: float32 [4, 1024], P(None, 'dp')
- m_in: float32 [1024, 10, 1024], P('dp', None, 'fsdp'), may hold values from -0.0004272461 to 0.0004272461
- m_out: float32 [6, 1024, 1024], P(None, 'fsdp', 'dp'), may hold values from -0.0004272461 to 0.0004272461
- m_vec: float32 [4, 1024], P(None, 'dp'), may hold values from -0.0012207031 to 0.0012207031
- v_in: float32 [1024, 10, 1024], P('dp', None, 'fsdp'), may hold values from 1.5685433e-09 to 2.5096693e-08
- v_out: float32 [6, 1024, 1024], P(None, 'fsdp', 'dp'), may hold values from 1.5685433e-09 to 2.5096693e-08
- v_vec: float32 [4, 1024], P(None, 'dp'), may hold values from 4.6748743e-09 to 7.947286e-08
Outputs:
- output: bfloat16 [16, 256, 1024], P('dp', 'fsdp')
- token_grad: bfloat16 [16, 256, 1024], P('dp', 'fsdp')
- grad_norm: float32 [], replicated
- new_w_in: float32 [1024, 10, 1024], P('dp', None, 'fsdp')
- new_w_out: float32 [6, 1024, 1024], P(None, 'fsdp', 'dp')
- new_vectors: float32 [4, 1024], P(None, 'dp')
- new_m_in: float32 [1024, 10, 1024], P('dp', None, 'fsdp')
- new_m_out: float32 [6, 1024, 1024], P(None, 'fsdp', 'dp')
- new_m_vec: float32 [4, 1024], P(None, 'dp')
- new_v_in: float32 [1024, 10, 1024], P('dp', None, 'fsdp')
- new_v_out: float32 [6, 1024, 1024], P(None, 'fsdp', 'dp')
- new_v_vec: float32 [4, 1024], P(None, 'dp')
Inputs may be any that keep to these rules, and one draw needn't show every extreme that they name: `masks`: each clip has its own masking rate, drawn between one half and 0.99; tokens are masked independently at that rate.
All inputs are finite; a program needn't handle non-finite values.
Results may differ from a plain program's by a relative error of at most 0.02.
The roundings to bfloat16 on the way count: a program that leaves them out, or rounds other values in their place, can miss the bound.
Values may be sent and summed in bfloat16 or wider, within the bound.
A program may use at most 128 MiB of HBM per device.

v0:
```python
import jax
import jax.numpy as jnp
from jax import lax
from jax.sharding import PartitionSpec as P

FRAMES = 16
STEP = 10
HDIM = 64


EPS_NORM = 1e-05
CLIP_AT = 1.0
BETA_FIRST = 0.9
BETA_SECOND = 0.95
ADAM_EPS = 1e-08
DECAY_RATE = 0.1
RATE_INPUT = 0.02
RATE_OUTPUT = 0.08
RATE_VECTOR = 1.0
NEG_FILL = -1e30


def from_behind(value, axis, steps):
    count = lax.axis_size(axis)
    first, last = (max(0, -steps), min(count, count - steps))
    return lax.ppermute(value, axis, [(source, source + steps) for source in range(first, last)])


def norm_parts(values):
    centered = values - jnp.mean(values, axis=-1, keepdims=True)
    rstd = lax.rsqrt(jnp.mean(centered * centered, axis=-1, keepdims=True) + EPS_NORM)
    return (centered * rstd, rstd)


def norm_back(grad_out, normed, rstd, gain):
    grad_hat = grad_out * gain
    first_mean = jnp.mean(grad_hat, axis=-1, keepdims=True)
    second_mean = jnp.mean(grad_hat * normed, axis=-1, keepdims=True)
    return (
        rstd * (grad_hat - first_mean - normed * second_mean),
        jnp.sum(grad_out * normed, axis=(0, 1)),
    )


def softmax_parts(scores, axis_at):
    peak = jnp.max(scores, axis=axis_at, keepdims=True)
    expd = jnp.exp(scores - peak)
    total = jnp.sum(expd, axis=axis_at, keepdims=True)
    return (expd / total, peak, total)


def spread_rows(values):
    return lax.all_gather(values, "fsdp", axis=1, tiled=True)


def collect_rows(partial_value):
    return lax.psum_scatter(partial_value, "fsdp", scatter_dimension=1, tiled=True)


def spread_grad(grad):
    return lax.all_gather(grad.astype(jnp.bfloat16), "fsdp", axis=1, tiled=True)


def collect_grad(partial_value):
    return lax.psum_scatter(
        partial_value.astype(jnp.bfloat16), "fsdp", scatter_dimension=1, tiled=True
    ).astype(jnp.float32)


def adamw_step(weight, first, second, grad, rate):
    first = BETA_FIRST * first + (1.0 - BETA_FIRST) * grad
    second = BETA_SECOND * second + (1.0 - BETA_SECOND) * grad * grad
    fix_first = 1.0 - BETA_FIRST**STEP
    fix_second = 1.0 - BETA_SECOND**STEP
    update = first / fix_first / (jnp.sqrt(second / fix_second) + ADAM_EPS)
    return (weight - rate * (update + DECAY_RATE * weight), first, second)


def local(tokens, masks, cotangent, w_in, w_out, vectors, m_in, m_out, m_vec, v_in, v_out, v_vec):
    f32 = jnp.float32
    b16 = jnp.bfloat16
    frames_here = tokens.shape[0]
    span_devices = FRAMES // frames_here
    heads_here = w_in.shape[2] // HDIM
    score_scale = HDIM ** (-0.5)
    wide_in, wide_out, small = (
        lax.all_gather(w_in.astype(b16), "dp", axis=0, tiled=True),
        lax.all_gather(w_out.astype(b16), "dp", axis=2, tiled=True),
        lax.all_gather(vectors.astype(b16), "dp", axis=1, tiled=True),
    )
    gains = small.astype(f32)
    embedded = jnp.where(masks[:, :, None] == 1, gains[3], tokens.astype(f32))
    hat_one, rstd_one = norm_parts(embedded)
    normed_one = spread_rows((hat_one * gains[0]).astype(b16))
    full_rows = normed_one.shape[1]
    heads_shape = (frames_here, full_rows, heads_here, HDIM)
    proj_one = jnp.einsum(
        "fsd,dcn->fscn", normed_one, wide_in[:, 0:3], preferred_element_type=f32
    ).astype(b16)
    query_one = proj_one[:, :, 0].reshape(heads_shape)
    key_one = proj_one[:, :, 1].reshape(heads_shape)
    value_one = proj_one[:, :, 2].reshape(heads_shape)
    scores_one = (
        jnp.einsum("fqhe,fkhe->fhqk", query_one, key_one, preferred_element_type=f32) * score_scale
    )
    probs_one, peak_one, total_one = softmax_parts(scores_one, 3)
    mixed_one = (
        jnp.einsum("fhqk,fkhe->fqhe", probs_one.astype(b16), value_one, preferred_element_type=f32)
        .astype(b16)
        .reshape(frames_here, full_rows, -1)
    )
    first_mid = embedded + collect_rows(
        jnp.einsum("fsn,nd->fsd", mixed_one, wide_out[0], preferred_element_type=f32)
    )
    hat_two, rstd_two = norm_parts(first_mid)
    normed_two = spread_rows((hat_two * gains[1]).astype(b16))
    proj_two = jnp.einsum(
        "fsd,dcn->fscn", normed_two, wide_in[:, 3:6], preferred_element_type=f32
    ).astype(b16)
    query_two = proj_two[:, :, 0].reshape(heads_shape)
    key_two = proj_two[:, :, 1].reshape(heads_shape)
    value_two = proj_two[:, :, 2].reshape(heads_shape)
    pair_here = jnp.stack([key_two, value_two])
    earlier = []
    for offset in range(span_devices - 1, 0, -1):
        earlier.append(from_behind(pair_here, "dp", offset))
    pair_all = jnp.concatenate(earlier + [pair_here], axis=1)
    clip_place = lax.axis_index("dp") % span_devices
    key_ids = (clip_place - span_devices + 1) * frames_here + jnp.arange(
        span_devices * frames_here, dtype=jnp.int32
    )
    query_ids = clip_place * frames_here + jnp.arange(frames_here, dtype=jnp.int32)
    allowed = ((key_ids[None, :] >= 0) & (key_ids[None, :] <= query_ids[:, None]))[None, :, :, None]
    scores_two = (
        jnp.einsum("fshe,gshe->hfgs", query_two, pair_all[0], preferred_element_type=f32)
        * score_scale
    )
    scores_two = jnp.where(allowed, scores_two, NEG_FILL)
    probs_two, peak_two, total_two = softmax_parts(scores_two, 2)
    mixed_two = (
        jnp.einsum(
            "hfgs,gshe->fshe", probs_two.astype(b16), pair_all[1], preferred_element_type=f32
        )
        .astype(b16)
        .reshape(frames_here, full_rows, -1)
    )
    second_mid = first_mid + collect_rows(
        jnp.einsum("fsn,nd->fsd", mixed_two, wide_out[1], preferred_element_type=f32)
    )
    hat_three, rstd_three = norm_parts(second_mid)
    normed_three = spread_rows((hat_three * gains[2]).astype(b16))
    pre_act = jnp.einsum(
        "fsd,dcn->fscn", normed_three, wide_in[:, 6:10], preferred_element_type=f32
    )
    activated = jax.nn.gelu(pre_act).astype(b16)
    result = second_mid + collect_rows(
        jnp.einsum("fscn,cnd->fsd", activated, wide_out[2:6], preferred_element_type=f32)
    )
    output = result.astype(b16)
    back_in, back_out = (
        lax.all_gather(w_in.astype(b16), "dp", axis=0, tiled=True),
        lax.all_gather(w_out.astype(b16), "dp", axis=2, tiled=True),
    )
    grad_result = cotangent.astype(f32)
    grad_three = spread_grad(grad_result)
    grad_act = jnp.einsum("fsd,cnd->fscn", grad_three, back_out[2:6], preferred_element_type=f32)
    grad_down = jnp.einsum("fscn,fsd->cnd", activated, grad_three, preferred_element_type=f32)
    gelu_value, gelu_pull = jax.vjp(jax.nn.gelu, pre_act)
    grad_pre = gelu_pull(grad_act)[0].astype(b16)
    grad_up = jnp.einsum("fsd,fscn->dcn", normed_three, grad_pre, preferred_element_type=f32)
    grad_normed_three = collect_grad(
        jnp.einsum("fscn,dcn->fsd", grad_pre, back_in[:, 6:10], preferred_element_type=f32)
    )
    back_three, gain_three = norm_back(grad_normed_three, hat_three, rstd_three, gains[2])
    carry_two = grad_result + back_three
    grad_two = spread_grad(carry_two)
    grad_mixed_two = (
        jnp.einsum("fsd,nd->fsn", grad_two, back_out[1], preferred_element_type=f32)
        .astype(b16)
        .reshape(heads_shape)
    )
    grad_tout = jnp.einsum("fsn,fsd->nd", mixed_two, grad_two, preferred_element_type=f32)
    grad_probs_two = jnp.einsum(
        "fshe,gshe->hfgs", grad_mixed_two, pair_all[1], preferred_element_type=f32
    )
    grad_values_all = jnp.einsum(
        "hfgs,fshe->gshe", probs_two.astype(b16), grad_mixed_two, preferred_element_type=f32
    )
    grad_scores_two = (
        probs_two * (grad_probs_two - jnp.sum(probs_two * grad_probs_two, axis=2, keepdims=True))
    ).astype(b16)
    grad_query_two = (
        jnp.einsum("hfgs,gshe->fshe", grad_scores_two, pair_all[0], preferred_element_type=f32)
        * score_scale
    ).astype(b16)
    grad_keys_all = (
        jnp.einsum("hfgs,fshe->gshe", grad_scores_two, query_two, preferred_element_type=f32)
        * score_scale
    )
    grad_pair = jnp.stack([grad_keys_all, grad_values_all])
    own_start = (span_devices - 1) * frames_here
    summed_pair = grad_pair[:, own_start:]
    for offset in range(1, span_devices):
        start_at = (span_devices - 1 - offset) * frames_here
        summed_pair = summed_pair + from_behind(
            grad_pair[:, start_at : start_at + frames_here].astype(jnp.bfloat16), "dp", -offset
        ).astype(jnp.float32)
    summed_pair = summed_pair.astype(b16)
    grad_proj_two = jnp.stack([grad_query_two, summed_pair[0], summed_pair[1]], axis=2).reshape(
        frames_here, full_rows, 3, -1
    )
    grad_tqkv = jnp.einsum("fsd,fscn->dcn", normed_two, grad_proj_two, preferred_element_type=f32)
    grad_normed_two = collect_grad(
        jnp.einsum("fscn,dcn->fsd", grad_proj_two, back_in[:, 3:6], preferred_element_type=f32)
    )
    back_two, gain_two = norm_back(grad_normed_two, hat_two, rstd_two, gains[1])
    carry_one = carry_two + back_two
    grad_one = spread_grad(carry_one)
    grad_mixed_one = (
        jnp.einsum("fsd,nd->fsn", grad_one, back_out[0], preferred_element_type=f32)
        .astype(b16)
        .reshape(heads_shape)
    )
    grad_sout = jnp.einsum("fsn,fsd->nd", mixed_one, grad_one, preferred_element_type=f32)
    again_one = (
        jnp.einsum("fqhe,fkhe->fhqk", query_one, key_one, preferred_element_type=f32) * score_scale
    )
    probs_again = jnp.exp(again_one - peak_one) / total_one
    grad_probs_one = jnp.einsum(
        "fqhe,fkhe->fhqk", grad_mixed_one, value_one, preferred_element_type=f32
    )
    grad_value_one = jnp.einsum(
        "fhqk,fqhe->fkhe", probs_again.astype(b16), grad_mixed_one, preferred_element_type=f32
    ).astype(b16)
    grad_scores_one = (
        probs_again
        * (grad_probs_one - jnp.sum(probs_again * grad_probs_one, axis=3, keepdims=True))
    ).astype(b16)
    grad_query_one = (
        jnp.einsum("fhqk,fkhe->fqhe", grad_scores_one, key_one, preferred_element_type=f32)
        * score_scale
    ).astype(b16)
    grad_key_one = (
        jnp.einsum("fhqk,fqhe->fkhe", grad_scores_one, query_one, preferred_element_type=f32)
        * score_scale
    ).astype(b16)
    grad_proj_one = jnp.stack([grad_query_one, grad_key_one, grad_value_one], axis=2).reshape(
        frames_here, full_rows, 3, -1
    )
    grad_sqkv = jnp.einsum("fsd,fscn->dcn", normed_one, grad_proj_one, preferred_element_type=f32)
    grad_normed_one = collect_grad(
        jnp.einsum("fscn,dcn->fsd", grad_proj_one, back_in[:, 0:3], preferred_element_type=f32)
    )
    back_one, gain_one = norm_back(grad_normed_one, hat_one, rstd_one, gains[0])
    carry_zero = carry_one + back_one
    is_masked = masks[:, :, None] == 1
    grad_embed = jnp.sum(jnp.where(is_masked, carry_zero, 0.0), axis=(0, 1))
    token_grad = jnp.where(is_masked, 0.0, carry_zero).astype(b16)
    grad_in_full = jnp.concatenate([grad_sqkv, grad_tqkv, grad_up], axis=1)
    grad_out_full = jnp.concatenate([grad_sout[None], grad_tout[None], grad_down], axis=0)
    grad_vec_full = jnp.stack([gain_one, gain_two, gain_three, grad_embed])
    grad_in, grad_out, grad_vec_part = (
        lax.psum_scatter(grad_in_full, "dp", scatter_dimension=0, tiled=True),
        lax.psum_scatter(grad_out_full, "dp", scatter_dimension=2, tiled=True),
        lax.psum_scatter(grad_vec_full, "dp", scatter_dimension=1, tiled=True),
    )
    grad_vec = lax.psum(grad_vec_part, "fsdp")
    local_squares = (
        jnp.sum(grad_in * grad_in)
        + jnp.sum(grad_out * grad_out)
        + jnp.sum(grad_vec * grad_vec) / lax.axis_size("fsdp")
    )
    grad_norm = jnp.sqrt(lax.psum(local_squares, ("dp", "fsdp")))
    factor = CLIP_AT / jnp.maximum(grad_norm, CLIP_AT)
    new_w_in, new_m_in, new_v_in = adamw_step(w_in, m_in, v_in, grad_in * factor, RATE_INPUT)
    new_w_out, new_m_out, new_v_out = adamw_step(
        w_out, m_out, v_out, grad_out * factor, RATE_OUTPUT
    )
    new_vectors, new_m_vec, new_v_vec = adamw_step(
        vectors, m_vec, v_vec, grad_vec * factor, RATE_VECTOR
    )
    return (
        output,
        token_grad,
        grad_norm,
        new_w_in,
        new_w_out,
        new_vectors,
        new_m_in,
        new_m_out,
        new_m_vec,
        new_v_in,
        new_v_out,
        new_v_vec,
    )


def solution(mesh):
    in_specs = (
        P("dp", "fsdp", None),
        P("dp", "fsdp"),
        P("dp", "fsdp", None),
        P("dp", None, "fsdp"),
        P(None, "fsdp", "dp"),
        P(None, "dp"),
        P("dp", None, "fsdp"),
        P(None, "fsdp", "dp"),
        P(None, "dp"),
        P("dp", None, "fsdp"),
        P(None, "fsdp", "dp"),
        P(None, "dp"),
    )
    out_specs = (
        P("dp", "fsdp", None),
        P("dp", "fsdp", None),
        P(),
        P("dp", None, "fsdp"),
        P(None, "fsdp", "dp"),
        P(None, "dp"),
        P("dp", None, "fsdp"),
        P(None, "fsdp", "dp"),
        P(None, "dp"),
        P("dp", None, "fsdp"),
        P(None, "fsdp", "dp"),
        P(None, "dp"),
    )
    return jax.shard_map(local, mesh=mesh, in_specs=in_specs, out_specs=out_specs, check_vma=False)
```

profile of v0, /device:TPU:0, one launch (start us, length us, event | category | flops | bytes accessed | tf_op | source)
XLA Modules:
  0.0 1238.5 jit_solution(16367950817282308726)
XLA Ops:
  8.1 22.2 %all_gather.29 = bf16[4,1024]{1,0:T(4,128)(2,1)S(1)} all-gather(bf16[4,128]{1,0:T(4,128)(2,1)S(1)} %convert_element_type.159), channel_id=1, replica_groups=mesh['dp'=8,'fsdp'=4] {'dp'}, dimensions={1}, use_global_device_ids=true | all-gather | bytes 9216 | tf_op jit(solution)/shard_map/all_gather | solution.py:89
  37.4 12.1 all-gather.9.cloned.1.call-done
  49.4 89.9 %all-gather.11.cloned.1.call-done = bf16[1024,10,256]{0,2,1:T(8,128)(2,1)} async-done(((bf16[128,10,256]{0,2,1:T(8,128)(2,1)}), bf16[1024,10,256]{0,2,1:T(8,128)(2,1)}) %all-gather.11.cloned.1.call-update) | async-done | bytes 5242896 | tf_op jit(solution)/shard_map/all_gather | solution.py:87
  146.2 57.0 %all-gather.13.cloned.1.call-done = bf16[6,256,1024]{2,1,0:T(8,128)(2,1)} async-done(((bf16[6,256,128]{2,1,0:T(8,128)(2,1)}), bf16[6,256,1024]{2,1,0:T(8,128)(2,1)}) %all-gather.13.cloned.1.call-update) | async-done | bytes 3145744 | tf_op jit(solution)/shard_map/all_gather | solution.py:88
  206.2 29.7 %reduce-scatter.12.cloned.1.call-done = f32[2,64,1024]{2,1,0:T(8,128)} async-done(((f32[2,256,1024]{2,1,0:T(8,128)}), f32[2,64,1024]{2,1,0:T(8,128)}) %reduce-scatter.12.cloned.1.call-update) | async-done | bytes 524304 | tf_op jit(solution)/shard_map/reduce_scatter | solution.py:57
  238.3 16.8 %all-gather.15.cloned.1.call-done = bf16[2,256,1024]{2,1,0:T(8,128)(2,1)} async-done(((bf16[2,64,1024]{2,1,0:T(8,128)(2,1)}), bf16[2,256,1024]{2,1,0:T(8,128)(2,1)}) %all-gather.15.cloned.1.call-update) | async-done | bytes 1048592 | tf_op jit(solution)/shard_map/all_gather | solution.py:53
  285.9 9.1 collective-permute-done.1
  346.4 37.3 %concatenate.11 = bf16[2,16,256,4,64]{4,1,2,3,0:T(8,128)(2,1)} concatenate(bf16[2,2,256,4,64]{4,1,2,3,0:T(2,128)(2,1)} %copy.168, bf16[2,2,256,4,64]{4,1,2,3,0:T(2,128)(2,1)} %copy.169, bf16[2,2,256,4,64]{4,1,2,3,0:T(2,128)(2,1)} %copy.170, bf16[2,2,256,4,64]{4,1,2,3,0:T(2,128)(2,1)} %copy.171, bf16[2,2,256,4,64]{4,1,2,3,0:T(2,128)(2,1)} %copy.172, ...), dimensions={1} | concatenate | bytes 8388608 | tf_op jit(solution)/shard_map/concatenate | solution.py:127
  405.2 53.0 %reduce-scatter.14.cloned.1.call-done = f32[2,64,1024]{2,1,0:T(8,128)} async-done(((f32[2,256,1024]{2,1,0:T(8,128)}), f32[2,64,1024]{2,1,0:T(8,128)}) %reduce-scatter.14.cloned.1.call-update) | async-done | bytes 524304 | tf_op jit(solution)/shard_map/reduce_scatter | solution.py:57
  461.3 16.1 %all-gather.17.cloned.1.call-done = bf16[2,256,1024]{2,1,0:T(8,128)(2,1)} async-done(((bf16[2,64,1024]{2,1,0:T(8,128)(2,1)}), bf16[2,256,1024]{2,1,0:T(8,128)(2,1)}) %all-gather.17.cloned.1.call-update) | async-done | bytes 1048592 | tf_op jit(solution)/shard_map/all_gather | solution.py:53
  482.0 13.8 %all-gather.19.cloned.1.call-done = bf16[2,256,1024]{2,1,0:T(8,128)(2,1)} async-done(((bf16[2,64,1024]{2,1,0:T(8,128)(2,1)}), bf16[2,256,1024]{2,1,0:T(8,128)(2,1)}) %all-gather.19.cloned.1.call-update) | async-done | bytes 1048592 | tf_op jit(solution)/shard_map/all_gather | solution.py:61
  505.5 25.0 %reduce-scatter.18.cloned.1.call-done = bf16[2,64,1024]{2,1,0:T(8,128)(2,1)} async-done(((bf16[2,256,1024]{2,1,0:T(8,128)(2,1)}), bf16[2,64,1024]{2,1,0:T(8,128)(2,1)}) %reduce-scatter.18.cloned.1.call-update) | async-done | bytes 262160 | tf_op jit(solution)/shard_map/reduce_scatter | solution.py:65
  535.1 15.5 %all-gather.21.cloned.1.call-done = bf16[2,256,1024]{2,1,0:T(8,128)(2,1)} async-done(((bf16[2,64,1024]{2,1,0:T(8,128)(2,1)}), bf16[2,256,1024]{2,1,0:T(8,128)(2,1)}) %all-gather.21.cloned.1.call-update) | async-done | bytes 1048592 | tf_op jit(solution)/shard_map/all_gather | solution.py:61
  605.1 44.8 %collective-permute-done.10 = bf16[2,2,256,4,64]{2,4,3,1,0:T(8,128)(2,1)S(1)} collective-permute-done((bf16[2,2,256,4,64]{2,4,3,1,0:T(8,128)(2,1)S(1)}, bf16[2,2,256,4,64]{2,4,3,1,0:T(8,128)(2,1)S(1)}, u32[]{:S(2)}, u32[]{:S(2)}) %collective-permute-start.10) | collective-permute-done | bytes 524320 | tf_op jit(solution)/shard_map/ppermute | solution.py:26
  651.2 22.1 %collective-permute-done.11 = bf16[2,2,256,4,64]{2,4,3,1,0:T(8,128)(2,1)S(1)} collective-permute-done((bf16[2,2,256,4,64]{2,4,3,1,0:T(8,128)(2,1)S(1)}, bf16[2,2,256,4,64]{2,4,3,1,0:T(8,128)(2,1)S(1)}, u32[]{:S(2)}, u32[]{:S(2)}) %collective-permute-start.11) | collective-permute-done | bytes 524320 | tf_op jit(solution)/shard_map/ppermute | solution.py:26
  678.7 16.4 %collective-permute-done.9 = bf16[2,2,256,4,64]{2,4,3,1,0:T(8,128)(2,1)} collective-permute-done((bf16[2,2,256,4,64]{2,4,3,1,0:T(8,128)(2,1)}, bf16[2,2,256,4,64]{2,4,3,1,0:T(8,128)(2,1)}, u32[]{:S(2)}, u32[]{:S(2)}) %collective-permute-start.9) | collective-permute-done | bytes 524320 | tf_op jit(solution)/shard_map/ppermute | solution.py:26
  708.4 15.7 %reduce-scatter.20.cloned.1.call-done = bf16[2,64,1024]{2,1,0:T(8,128)(2,1)} async-done(((bf16[2,256,1024]{2,1,0:T(8,128)(2,1)}), bf16[2,64,1024]{2,1,0:T(8,128)(2,1)}) %reduce-scatter.20.cloned.1.call-update) | async-done | bytes 262160 | tf_op jit(solution)/shard_map/reduce_scatter | solution.py:65
  725.4 32.5 %reduce-scatter.16.cloned.1.call-done = f32[2,64,1024]{2,1,0:T(8,128)} async-done(((f32[2,256,1024]{2,1,0:T(8,128)}), f32[2,64,1024]{2,1,0:T(8,128)}) %reduce-scatter.16.cloned.1.call-update) | async-done | bytes 524304 | tf_op jit(solution)/shard_map/reduce_scatter | solution.py:57
  760.5 16.8 %all-gather.23.cloned.1.call-done = bf16[2,256,1024]{2,1,0:T(8,128)(2,1)} async-done(((bf16[2,64,1024]{2,1,0:T(8,128)(2,1)}), bf16[2,256,1024]{2,1,0:T(8,128)(2,1)}) %all-gather.23.cloned.1.call-update) | async-done | bytes 1048592 | tf_op jit(solution)/shard_map/all_gather | solution.py:61
  794.2 16.9 %reduce-scatter.22.cloned.1.call-done = bf16[2,64,1024]{2,1,0:T(8,128)(2,1)} async-done(((bf16[2,256,1024]{2,1,0:T(8,128)(2,1)}), bf16[2,64,1024]{2,1,0:T(8,128)(2,1)}) %reduce-scatter.22.cloned.1.call-update) | async-done | bytes 262160 | tf_op jit(solution)/shard_map/reduce_scatter | solution.py:65
  842.0 35.5 %reduce-scatter.28.cloned.1.call-done = f32[128,4]{1,0:T(8,128)} async-done(((f32[1024,4]{1,0:T(8,128)}), f32[128,4]{1,0:T(8,128)}) %reduce-scatter.28.cloned.1.call-update) | async-done | bytes 2064
  885.3 113.6 %reduce-scatter.26.cloned.1.call-done = f32[6,256,128]{2,1,0:T(8,128)} async-done(((f32[6,256,1024]{2,1,0:T(8,128)}), f32[6,256,128]{2,1,0:T(8,128)}) %reduce-scatter.26.cloned.1.call-update) | async-done | bytes 786448 | tf_op jit(solution)/shard_map/reduce_scatter | solution.py:264
  1000.8 179.5 %reduce-scatter.24.cloned.1.call-done = f32[128,10,256]{2,0,1:T(8,128)} async-done(((f32[1024,10,256]{2,0,1:T(8,128)}), f32[128,10,256]{2,0,1:T(8,128)}) %reduce-scatter.24.cloned.1.call-update) | async-done | bytes 1310736 | tf_op jit(solution)/shard_map/reduce_scatter | solution.py:263
  1183.9 39.4 %psum.15 = f32[]{:T(128)} all-reduce(f32[]{:T(128)S(6)} %add.203), channel_id=1, replica_groups=mesh['dp'=8,'fsdp'=4] {'dp','fsdp'}, use_global_device_ids=true, to_apply=%region_35.36 | all-reduce | flops 1 | bytes 8 | tf_op jit(solution)/shard_map/psum | solution.py:273
  (302 shorter events, 289.0 us)
Async XLA Ops:
  7.2 42.2 %all-gather.9.cloned.1.call-start = ((), (), s32[]{:S(2)}) async-start(), calls=%async_computation.9 | async-start | bytes 1310720 | tf_op jit(solution)/shard_map/all_gather | solution.py:53
  35.3 104.0 %all-gather.11.cloned.1.call-start = ((), (), s32[]{:S(2)}) async-start(), calls=%async_computation.10 | async-start | bytes 5898240 | tf_op jit(solution)/shard_map/all_gather | solution.py:87
  36.4 166.8 %all-gather.13.cloned.1.call-start = ((), (), s32[]{:S(2)}) async-start(), calls=%async_computation.11 | async-start | bytes 3538944 | tf_op jit(solution)/shard_map/all_gather | solution.py:88
  37.3 198.6 %reduce-scatter.12.cloned.1.call-start = ((), (), s32[]{:S(2)}) async-start(), calls=%async_computation.12 | async-start | bytes 2621440 | tf_op jit(solution)/shard_map/reduce_scatter | solution.py:57
  206.1 49.0 %all-gather.15.cloned.1.call-start = ((), (), s32[]{:S(2)}) async-start(), calls=%async_computation.13 | async-start | bytes 1310720 | tf_op jit(solution)/shard_map/all_gather | solution.py:53
  238.3 220.0 %reduce-scatter.14.cloned.1.call-start = ((), (), s32[]{:S(2)}) async-start(), calls=%async_computation.14 | async-start | bytes 2621440 | tf_op jit(solution)/shard_map/reduce_scatter | solution.py:57
  278.2 50.6 %collective-permute-start.4 = (bf16[2,2,256,4,64]{2,4,3,1,0:T(8,128)(2,1)}, bf16[2,2,256,4,64]{2,4,3,1,0:T(8,128)(2,1)}, u32[]{:S(2)}, u32[]{:S(2)}) collective-permute-start(bf16[2,2,256,4,64]{2,4,3,1,0:T(8,128)(2,1)} %copy.161), channel_id=1, source_target_pairs={{0,12},{4,16},{8,20},{12,24},{16,28},{1,13},{5,17},{9,21},{13,25},... | collective-permute-start | bytes 1572872 | tf_op jit(solution)/shard_map/ppermute | solution.py:26
  283.8 55.5 %collective-permute-start.5 = (bf16[2,2,256,4,64]{2,4,3,1,0:T(8,128)(2,1)}, bf16[2,2,256,4,64]{2,4,3,1,0:T(8,128)(2,1)}, u32[]{:S(2)}, u32[]{:S(2)}) collective-permute-start(bf16[2,2,256,4,64]{2,4,3,1,0:T(8,128)(2,1)} %copy.161), channel_id=1, source_target_pairs={{0,8},{4,12},{8,16},{12,20},{16,24},{20,28},{1,9},{5,13},{9,17},{1... | collective-permute-start | bytes 1572872 | tf_op jit(solution)/shard_map/ppermute | solution.py:26
  295.0 47.9 %collective-permute-start.6 = (bf16[2,2,256,4,64]{2,4,3,1,0:T(8,128)(2,1)}, bf16[2,2,256,4,64]{2,4,3,1,0:T(8,128)(2,1)}, u32[]{:S(2)}, u32[]{:S(2)}) collective-permute-start(bf16[2,2,256,4,64]{2,4,3,1,0:T(8,128)(2,1)} %copy.161), channel_id=1, source_target_pairs={{0,4},{4,8},{8,12},{12,16},{16,20},{20,24},{24,28},{1,5},{5,9},{9,... | collective-permute-start | bytes 1572872 | tf_op jit(solution)/shard_map/ppermute | solution.py:26
  405.2 72.3 %all-gather.17.cloned.1.call-start = ((), (), s32[]{:S(2)}) async-start(), calls=%async_computation.15 | async-start | bytes 1310720 | tf_op jit(solution)/shard_map/all_gather | solution.py:53
  461.3 69.2 %reduce-scatter.18.cloned.1.call-start = ((), (), s32[]{:S(2)}) async-start(), calls=%async_computation.18 | async-start | bytes 1310720 | tf_op jit(solution)/shard_map/reduce_scatter | solution.py:65
  505.5 45.1 %all-gather.21.cloned.1.call-start = ((), (), s32[]{:S(2)}) async-start(), calls=%async_computation.19 | async-start | bytes 1310720 | tf_op jit(solution)/shard_map/all_gather | solution.py:61
  533.7 190.4 %reduce-scatter.20.cloned.1.call-start = ((), (), s32[]{:S(2)}) async-start(), calls=%async_computation.20 | async-start | bytes 1310720 | tf_op jit(solution)/shard_map/reduce_scatter | solution.py:65
  598.3 51.6 %collective-permute-start.10 = (bf16[2,2,256,4,64]{2,4,3,1,0:T(8,128)(2,1)S(1)}, bf16[2,2,256,4,64]{2,4,3,1,0:T(8,128)(2,1)S(1)}, u32[]{:S(2)}, u32[]{:S(2)}) collective-permute-start(bf16[2,2,256,4,64]{2,4,3,1,0:T(8,128)(2,1)S(1)} %get-tuple-element.43), channel_id=1, source_target_pairs={{16,0},{20,4},{24,8},{28,12},{17,1},{21,5},{25,9},{29,13},{18,2},{... | collective-permute-start | bytes 1572872 | tf_op jit(solution)/shard_map/ppermute | solution.py:26
  599.9 73.4 %collective-permute-start.11 = (bf16[2,2,256,4,64]{2,4,3,1,0:T(8,128)(2,1)S(1)}, bf16[2,2,256,4,64]{2,4,3,1,0:T(8,128)(2,1)S(1)}, u32[]{:S(2)}, u32[]{:S(2)}) collective-permute-start(bf16[2,2,256,4,64]{2,4,3,1,0:T(8,128)(2,1)S(1)} %get-tuple-element.42), channel_id=1, source_target_pairs={{20,0},{24,4},{28,8},{21,1},{25,5},{29,9},{22,2},{26,6},{30,10},{2... | collective-permute-start | bytes 1572872 | tf_op jit(solution)/shard_map/ppermute | solution.py:26
  601.2 77.5 %collective-permute-start.12 = (bf16[2,2,256,4,64]{2,4,3,1,0:T(8,128)(2,1)}, bf16[2,2,256,4,64]{2,4,3,1,0:T(8,128)(2,1)}, u32[]{:S(2)}, u32[]{:S(2)}) collective-permute-start(bf16[2,2,256,4,64]{2,4,3,1,0:T(8,128)(2,1)} %get-tuple-element.41), channel_id=1, source_target_pairs={{24,0},{28,4},{25,1},{29,5},{26,2},{30,6},{27,3},{31,7}} | collective-permute-start | bytes 1572872 | tf_op jit(solution)/shard_map/ppermute | solution.py:26
  602.5 76.2 %collective-permute-start.13 = (bf16[2,2,256,4,64]{2,4,3,1,0:T(8,128)(2,1)}, bf16[2,2,256,4,64]{2,4,3,1,0:T(8,128)(2,1)}, u32[]{:S(2)}, u32[]{:S(2)}) collective-permute-start(bf16[2,2,256,4,64]{2,4,3,1,0:T(8,128)(2,1)} %get-tuple-element.40), channel_id=1, source_target_pairs={{28,0},{29,1},{30,2},{31,3}} | collective-permute-start | bytes 1572872 | tf_op jit(solution)/shard_map/ppermute | solution.py:26
  603.8 74.9 %collective-permute-start.7 = (bf16[2,2,256,4,64]{2,4,3,1,0:T(8,128)(2,1)}, bf16[2,2,256,4,64]{2,4,3,1,0:T(8,128)(2,1)}, u32[]{:S(2)}, u32[]{:S(2)}) collective-permute-start(bf16[2,2,256,4,64]{2,4,3,1,0:T(8,128)(2,1)} %get-tuple-element.39), channel_id=1, source_target_pairs={{4,0},{8,4},{12,8},{16,12},{20,16},{24,20},{28,24},{5,1},{9,5},{13... | collective-permute-start | bytes 1572872 | tf_op jit(solution)/shard_map/ppermute | solution.py:26
  702.7 55.2 %reduce-scatter.16.cloned.1.call-start = ((), (), s32[]{:S(2)}) async-start(), calls=%async_computation.16 | async-start | bytes 2621440 | tf_op jit(solution)/shard_map/reduce_scatter | solution.py:57
  708.4 69.0 %all-gather.23.cloned.1.call-start = ((), (), s32[]{:S(2)}) async-start(), calls=%async_computation.21 | async-start | bytes 1310720 | tf_op jit(solution)/shard_map/all_gather | solution.py:61
  760.5 50.6 %reduce-scatter.22.cloned.1.call-start = ((), (), s32[]{:S(2)}) async-start(), calls=%async_computation.22 | async-start | bytes 1310720 | tf_op jit(solution)/shard_map/reduce_scatter | solution.py:65
  786.1 91.4 %reduce-scatter.28.cloned.1.call-start = ((), (), s32[]{:S(2)}) async-start(), calls=%async_computation.25 | async-start | bytes 589824
  815.5 183.4 %reduce-scatter.26.cloned.1.call-start = ((), (), s32[]{:S(2)}) async-start(), calls=%async_computation.24 | async-start | bytes 7077888 | tf_op jit(solution)/shard_map/reduce_scatter | solution.py:264
  821.7 358.6 %reduce-scatter.24.cloned.1.call-start = ((), (), s32[]{:S(2)}) async-start(), calls=%async_computation.23 | async-start | bytes 11796480 | tf_op jit(solution)/shard_map/reduce_scatter | solution.py:263
  (70 other events, 2979.6 us)
Sparse Core Ops, SparseCore 0:
  35.4 14.0 all-gather.8
  52.0 87.2 all-gather.10
  141.9 61.2 all-gather.12
  206.2 29.5 reduce-scatter.11
  238.4 16.7 all-gather.14
  405.3 52.9 reduce-scatter.13
  460.6 16.7 all-gather.16
  479.0 16.7 all-gather.18
  505.6 24.8 reduce-scatter.17
  533.8 16.7 all-gather.20
  702.8 21.2 reduce-scatter.19
  726.5 31.3 reduce-scatter.15
  760.6 16.7 all-gather.22
  786.2 24.8 reduce-scatter.21
  815.6 61.8 reduce-scatter.27
  881.4 117.4 reduce-scatter.25
  1002.7 177.5 reduce-scatter.23
where the time goes:
time: 1250 us; the launch traced here: 1240 us
  waiting for transfers between devices  859 us (69%)
  local copies, waits for them, and re-layouts  112 us (9%)
  matrix products  86.9 us (7%)
  blocking collectives  67.3 us (5%)
  other arithmetic  64.7 us (5%)
  starting transfers between devices  30.4 us (2%)
  between operations  18.9 us (2%)
    reduce_scatter x1, waiting for transfers between devices, local(): lax.psum_scatter(grad_in_full, 'dp', scatter_dimension=0, tiled=True)  180 us
    ppermute x14, waiting for transfers between devices, from_behind(): lax.ppermute(value, axis, [(source, source + steps) for source in range(f...  118 us
    reduce_scatter x3, waiting for transfers between devices, collect_rows(): lax.psum_scatter(partial_value, 'fsdp', scatter_dimension=1, tiled=True)  115 us
    reduce_scatter x1, waiting for transfers between devices, local(): lax.psum_scatter(grad_out_full, 'dp', scatter_dimension=2, tiled=True)  114 us
    all_gather x1, waiting for transfers between devices, local(): lax.all_gather(w_in.astype(b16), 'dp', axis=0, tiled=True)  89.9 us
    reduce_scatter x3, waiting for transfers between devices, collect_grad(): lax.psum_scatter(partial_value.astype(jnp.bfloat16), 'fsdp', scatter_dime...  57.6 us
    all_gather x1, waiting for transfers between devices, local(): lax.all_gather(w_out.astype(b16), 'dp', axis=2, tiled=True)  57 us
    all_gather x3, waiting for transfers between devices, spread_grad(): return lax.all_gather(grad.astype(jnp.bfloat16), 'fsdp', axis=1, tiled=True)  46.1 us
  transfers between devices with their start and end apart: 31, of which 26 were waited for; matrix products, arithmetic and copies ran while one was open for 7% of the time, Pallas kernels for 0%

commit v1 on v0

v1 whole, which is shorter than its diff:
```python
import functools
from types import SimpleNamespace

import jax
import jax.numpy as jnp
from jax import lax
from jax.experimental import pallas as pl
from jax.experimental.pallas import tpu as pltpu
from jax.sharding import PartitionSpec as P

FRAMES = 16
STEP = 10
HDIM = 64


EPS_NORM = 1e-05
CLIP_AT = 1.0
BETA_FIRST = 0.9
BETA_SECOND = 0.95
ADAM_EPS = 1e-08
DECAY_RATE = 0.1
RATE_INPUT = 0.02
RATE_OUTPUT = 0.08
RATE_VECTOR = 1.0
NEG_FILL = -1e30
GELU_A = 0.7978845608028654
GELU_B = 0.044715

F32 = jnp.float32
B16 = jnp.bfloat16
MESH = pl.DeviceIdType.MESH
CHUNK = 16
DP = "dp"
TP = "fsdp"
LANES = 128
VMEM_BYTES = 63 << 20


def at(dp, fsdp):
    return {DP: dp, TP: fsdp}


def nn(a, b):
    return lax.dot_general(a, b, (((1,), (0,)), ((), ())), preferred_element_type=F32)


def nt(a, b):
    return lax.dot_general(a, b, (((1,), (1,)), ((), ())), preferred_element_type=F32)


def tn(a, b):
    return lax.dot_general(a, b, (((0,), (0,)), ((), ())), preferred_element_type=F32)


def loop(low, high, step):
    def body(k, carry):
        step(k)
        return carry

    lax.fori_loop(low, high, body, 0)


def each(low, high, step):
    if high - low <= 8:
        for k in range(low, high):
            step(k)
    else:
        loop(low, high, step)


def scratch_of(z):
    rows, width, hidden, span = z.rows, z.width, z.hidden, z.span
    nd, nf, part, heads = z.nd, z.nf, z.part, z.heads
    outer = nd // 2
    flat = (nf, z.frames, z.here, hidden)
    vmem = pltpu.VMEM
    dma = pltpu.SemaphoreType.DMA
    return dict(
        weights=vmem((4, 4, width, hidden), B16),
        gathered=vmem((6, nf, rows, width), B16),
        gains=vmem((8, width), F32),
        tiles=vmem((nd, 8, LANES), F32),
        hats=vmem((3, rows, width), F32),
        rstds=vmem((3, rows, LANES), F32),
        work=vmem((rows, width), F32),
        mid=vmem((rows, width), F32),
        swap_out=vmem((5, span, CHUNK, width), B16),
        swap_in=vmem((5, span, CHUNK, width), B16),
        part_sum=vmem((2, 2, rows, width), F32),
        sib_out=vmem((2, 2, rows, width), B16),
        sib_in=vmem((2, 2, rows, width), B16),
        far_out=vmem((2, rows, width), B16),
        far_in=vmem((2, rows, width), B16),
        qkv=vmem((2, 3) + flat, B16),
        mixed=vmem((2,) + flat, B16),
        grad_mixed=vmem(flat, B16),
        grad_qkv=vmem((3,) + flat, B16),
        probs_a=vmem((z.frames * heads, nf * z.here, nf * z.here), F32),
        probs_b=vmem((nf * heads, rows, rows), F32),
        act=vmem((4,) + flat, B16),
        slope=vmem((4,) + flat, F32),
        grad_pre=vmem((4,) + flat, B16),
        product=vmem((outer, 2, part, hidden), F32),
        own_sum=vmem((16, outer, part, hidden), B16),
        pair_out=vmem((16, outer, part, hidden), B16),
        pair_in=vmem((16, outer, part, hidden), B16),
        line_in=vmem((16, outer, part, hidden), B16),
        vec_acc=vmem((8, width), F32),
        vec_out=vmem((width // LANES, 8, LANES), F32),
        vec_in=vmem((nd, 8, LANES), F32),
        vec_mine=vmem((8, LANES), F32),
        vec_side=vmem((nf, 8, LANES), F32),
        sq_mine=vmem((2, 8, LANES), F32),
        sq_side=vmem((nf, 8, LANES), F32),
        sq_all=vmem((nd, 8, LANES), F32),
        small_s=dma((5,)),
        small_r=dma((5,)),
        line_ws=dma((4,)),
        line_wr=dma((4, outer)),
        pair_ws=dma((4,)),
        pair_wr=dma((4,)),
        copy_w=dma((4,)),
        row_s=dma((6, 3)),
        row_r=dma((6, 3)),
        sum_s=dma((6, 3)),
        sum_r=dma((6, 3)),
        swap_s=dma((5,)),
        swap_r=dma((5,)),
        pair_gs=dma((16,)),
        pair_gr=dma((16,)),
        line_gs=dma((16,)),
        line_gr=dma((16,)),
    )


def layer(z, names, *refs):
    tok, msk, cot, shard, vec = refs[:5]
    out, tgr, nrm, gout, gvec = refs[5:10]
    s = SimpleNamespace(**dict(zip(names, refs[10:])))
    rows, width, hidden, span = z.rows, z.width, z.hidden, z.span
    nd, nf, part, heads = z.nd, z.nf, z.part, z.heads
    frames, here = z.frames, z.here
    outer = nd // 2
    piece = here // span
    n_pairs = heads // 2
    scale = HDIM**-0.5
    gathered, weights, gains = s.gathered, s.weights, s.gains
    work, mid = s.work, s.mid
    swap_out, swap_in = s.swap_out, s.swap_in

    d, f = lax.axis_index(DP), lax.axis_index(TP)
    o, i = d // 2, d % 2
    y, c = f // 2, f % 2
    place = d % span
    base = d - place
    f_sib, f_far, f_last = y * 2 + 1 - c, (1 - y) * 2 + c, (1 - y) * 2 + 1 - c
    mate = at(o * 2 + 1 - i, f)
    sib = at(d, f_sib)
    far = at(d, f_far)

    def rcopy(src, dst, ssem, rsem, dev):
        return pltpu.make_async_remote_copy(
            src_ref=src, dst_ref=dst, send_sem=ssem, recv_sem=rsem, device_id=dev, device_id_type=MESH
        )

    bar = pltpu.get_barrier_semaphore()

    def greet(q):
        dev = at((d + q) % nd, f)
        pl.semaphore_signal(bar, inc=1, device_id=dev, device_id_type=MESH)

    each(1, nd, greet)
    for q in range(1, nf):
        dev = at(d, (f + q) % nf)
        pl.semaphore_signal(bar, inc=1, device_id=dev, device_id_type=MESH)
    pl.semaphore_wait(bar, nd - 1 + nf - 1)

    def tell(n, src_of, dst, axis):
        count, me = (nd, d) if axis == DP else (nf, f)

        def go(q):
            to = (me + q) % count
            dev = at(to, f) if axis == DP else at(d, to)
            rcopy(src_of(to), dst.at[me], s.small_s.at[n], s.small_r.at[n], dev).start()

        each(1, count, go)

    def hear(n, dst, axis):
        count = nd if axis == DP else nf
        others = dst.at[pl.ds(0, count - 1)]
        cp = rcopy(others, others, s.small_s.at[n], s.small_r.at[n], mate)
        cp.wait_recv()
        cp.wait_send()

    def total_of(ref, count):
        total = ref[0]
        if count <= 8:
            for k in range(1, count):
                total = total + ref[k]
            return total
        return lax.fori_loop(1, count, lambda k, t: t + ref[k], total)

    tell(0, lambda to: vec, s.tiles, DP)

    def shard_rows(owner):
        return pl.ds(pl.multiple_of(owner * part, part), part)

    def gather_start(g):
        mine = weights.at[g, :, shard_rows(d), :]
        pltpu.make_async_copy(shard.at[g], mine, s.copy_w.at[g]).start()

        def go(q):
            dev = at(((o + q) % outer) * 2 + i, f)
            rcopy(shard.at[g], mine, s.line_ws.at[g], s.line_wr.at[g, q], dev).start()

        each(1, outer, go)
        rcopy(shard.at[g], mine, s.pair_ws.at[g], s.pair_wr.at[g], mate).start()

    def gather_pass(g):
        def go(q):
            block = weights.at[g, :, shard_rows(((o + outer - q) % outer) * 2 + i), :]
            rcopy(block, block, s.line_ws.at[g], s.line_wr.at[g, q], mate).wait_recv()
            rcopy(block, block, s.pair_ws.at[g], s.pair_wr.at[g], mate).start()

        each(1, outer, go)

    def gather_ready(g):
        mine = weights.at[g, :, shard_rows(d), :]
        pltpu.make_async_copy(shard.at[g], mine, s.copy_w.at[g]).wait()
        half = weights.at[g, :, pl.ds(0, outer * part), :]
        rcopy(half, half, s.pair_ws.at[g], s.pair_wr.at[g], mate).wait_recv()

    def gather_end(g):
        half = weights.at[g, :, pl.ds(0, outer * part), :]
        rcopy(half, half, s.pair_ws.at[g], s.pair_wr.at[g], mate).wait_send()
        rest = weights.at[g, :, pl.ds(0, (outer - 1) * part), :]
        rcopy(rest, rest, s.line_ws.at[g], s.line_wr.at[g, 0], mate).wait_send()

    def spread_start(k):
        block = gathered.at[k, f]
        rcopy(block, block, s.row_s.at[k, 1], s.row_r.at[k, 1], far).start()
        rcopy(block, block, s.row_s.at[k, 0], s.row_r.at[k, 0], sib).start()

    def spread_near(k):
        block = gathered.at[k, f_sib]
        rcopy(block, block, s.row_s.at[k, 0], s.row_r.at[k, 0], sib).wait_recv()

    def spread_pass(k):
        block = gathered.at[k, f_far]
        rcopy(block, block, s.row_s.at[k, 1], s.row_r.at[k, 1], far).wait_recv()
        rcopy(block, block, s.row_s.at[k, 2], s.row_r.at[k, 2], sib).start()

    def spread_far(k):
        block = gathered.at[k, f_last]
        rcopy(block, block, s.row_s.at[k, 2], s.row_r.at[k, 2], sib).wait_recv()

    def spread_end(k):
        block = gathered.at[k, f]
        for n in range(3):
            rcopy(block, block, s.row_s.at[k, n], s.row_r.at[k, n], sib).wait_send()

    def collect_start(k, terms):
        par = k % 2
        for slot in range(2):
            pair = (1 - y) if slot == 0 else y

            def tile(t, slot=slot, pair=pair):
                cols = pl.ds(pl.multiple_of(t * hidden, hidden), hidden)
                total = None
                for b_ref, g, j in terms:
                    value = nt(
                        b_ref[pl.ds(pair * 2, 2)].reshape(2 * rows, hidden), weights[g, j, cols, :]
                    )
                    total = value if total is None else total + value
                s.part_sum[slot, :, :, cols] = total.reshape(2, rows, hidden)

            loop(0, width // hidden, tile)
            s.sib_out[par, slot] = s.part_sum[slot, 1 - c].astype(B16)
            rcopy(
                s.sib_out.at[par, slot],
                s.sib_in.at[par, slot],
                s.sum_s.at[k, slot],
                s.sum_r.at[k, slot],
                sib,
            ).start()
        back = s.sib_in.at[par, 0]
        rcopy(back, back, s.sum_s.at[k, 0], s.sum_r.at[k, 0], sib).wait_recv()
        s.far_out[par] = (s.part_sum[0, c] + s.sib_in[par, 0].astype(F32)).astype(B16)
        rcopy(
            s.far_out.at[par], s.far_in.at[par], s.sum_s.at[k, 2], s.sum_r.at[k, 2], far
        ).start()

    def collect_end(k):
        par = k % 2
        near, away = s.sib_in.at[par, 1], s.far_in.at[par]
        rcopy(near, near, s.sum_s.at[k, 1], s.sum_r.at[k, 1], sib).wait_recv()
        rcopy(away, away, s.sum_s.at[k, 2], s.sum_r.at[k, 2], far).wait_recv()
        for n in range(3):
            rcopy(near, near, s.sum_s.at[k, n], s.sum_r.at[k, n], sib).wait_send()

        def get(block):
            return (
                s.part_sum[1, c, block]
                + s.sib_in[par, 1, block].astype(F32)
                + s.far_in[par, block].astype(F32)
            )

        return get

    def swap_start(k):
        def go(q):
            to = (place + q) % span
            rcopy(
                swap_out.at[k, to],
                swap_in.at[k, place],
                s.swap_s.at[k],
                s.swap_r.at[k],
                at(base + to, f),
            ).start()

        each(1, span, go)
        swap_in[k, place] = swap_out[k, place]

    def swap_wait(k):
        others = swap_in.at[k, pl.ds(0, span - 1)]
        rcopy(others, others, s.swap_s.at[k], s.swap_r.at[k], mate).wait_recv()

    def swap_end(k):
        others = swap_in.at[k, pl.ds(0, span - 1)]
        rcopy(others, others, s.swap_s.at[k], s.swap_r.at[k], mate).wait_send()

    def token_rows(fr, j):
        return pl.ds(pl.multiple_of(fr * here + j * piece, piece), piece)

    def pack(k, src):
        def step(j):
            parts = [src[token_rows(fr, j), :] for fr in range(frames)]
            swap_out[k, j] = jnp.concatenate(parts, axis=0).astype(B16)

        loop(0, span, step)

    def unpack(k, dst):
        def step(j):
            value = swap_in[k, j].astype(F32)
            for fr in range(frames):
                dst[token_rows(fr, j), :] = value[fr * piece : (fr + 1) * piece]

        loop(0, span, step)

    def chunks(step):
        loop(0, rows // CHUNK, lambda k: step(pl.ds(pl.multiple_of(k * CHUNK, CHUNK), CHUNK), k))

    def norm_rows(n, value, block):
        centered = value - jnp.mean(value, axis=-1, keepdims=True)
        rstd = lax.rsqrt(jnp.mean(centered * centered, axis=-1, keepdims=True) + EPS_NORM)
        hat = centered * rstd
        s.hats[n, block] = hat
        s.rstds[n, block] = jnp.broadcast_to(rstd, (CHUNK, LANES))
        return (hat * gains[n : n + 1, :]).astype(B16)

    def norm_back(n, grad, block):
        hat = s.hats[n, block]
        rstd = s.rstds[n, block][:, 0:1]
        grad_hat = grad * gains[n : n + 1, :]
        first = jnp.mean(grad_hat, axis=-1, keepdims=True)
        second = jnp.mean(grad_hat * hat, axis=-1, keepdims=True)
        s.vec_acc[n : n + 1, :] += jnp.sum(grad * hat, axis=0, keepdims=True)
        return rstd * (grad_hat - first - hat * second)

    def pair_rows(k, pair):
        return gathered[k, pl.ds(pair * 2, 2)].reshape(2 * rows, width)

    def as_flat(value):
        return value.reshape(2, frames, here, hidden)

    def project(k, g, dst, pair):
        def step(j):
            dst[j, pl.ds(pair * 2, 2)] = as_flat(nn(pair_rows(k, pair), weights[g, j]).astype(B16))

        loop(0, 3, step)

    def attend(block):
        spatial = block == 0
        n = nf * here if spatial else rows

        def load(ref, g, lanes):
            value = ref[:, g, :, lanes] if spatial else ref[g, :, :, lanes]
            return value.reshape(n, 2 * HDIM)

        def store(ref, g, lanes, value):
            if spatial:
                ref[:, g, :, lanes] = value.reshape(nf, here, 2 * HDIM)
            else:
                ref[g, :, :, lanes] = value.reshape(frames, here, 2 * HDIM)

        return n, load, store, (s.probs_a if spatial else s.probs_b)

    def head_lanes(n):
        return lax.broadcasted_iota(jnp.int32, (n, 2 * HDIM), 1) < HDIM

    def kept(n):
        query = lax.broadcasted_iota(jnp.int32, (n, n), 0)
        key = lax.broadcasted_iota(jnp.int32, (n, n), 1)
        return (query % piece == key % piece) & (key // piece <= query // piece)

    def each_pair(block, step):
        def go(k):
            lanes = pl.ds(pl.multiple_of((k % n_pairs) * 2 * HDIM, 2 * HDIM), 2 * HDIM)
            step(k, k // n_pairs, lanes)

        loop(0, (frames if block == 0 else nf) * n_pairs, go)

    def attention(block):
        n, load, store, probs = attend(block)
        qkv = s.qkv.at[block]

        def step(k, g, lanes):
            query, key, value = (load(qkv.at[j], g, lanes) for j in range(3))
            low = head_lanes(n)
            found = []
            for h in range(2):
                mine = jnp.where(low if h == 0 else ~low, query, jnp.zeros_like(query))
                scores = nt(mine, key) * scale
                if block == 1:
                    scores = jnp.where(kept(n), scores, NEG_FILL)
                expd = jnp.exp(scores - jnp.max(scores, axis=-1, keepdims=True))
                prob = expd / jnp.sum(expd, axis=-1, keepdims=True)
                probs[k * 2 + h] = prob
                found.append(nn(prob.astype(B16), value))
            store(s.mixed.at[block], g, lanes, jnp.where(low, found[0], found[1]).astype(B16))

        each_pair(block, step)

    def attention_back(block):
        n, load, store, probs = attend(block)
        qkv = s.qkv.at[block]

        def step(k, g, lanes):
            query, key, value = (load(qkv.at[j], g, lanes) for j in range(3))
            grad = load(s.grad_mixed, g, lanes)
            low = head_lanes(n)
            found = []
            for h in range(2):
                mine = jnp.where(low if h == 0 else ~low, grad, jnp.zeros_like(grad))
                prob = probs[k * 2 + h]
                grad_prob = nt(mine, value)
                inner = jnp.sum(prob * grad_prob, axis=-1, keepdims=True)
                grad_score = (prob * (grad_prob - inner)).astype(B16)
                found.append(
                    (
                        nn(grad_score, key) * scale,
                        tn(grad_score, query) * scale,
                        tn(prob.astype(B16), grad),
                    )
                )
            for j in range(3):
                both = jnp.where(low, found[0][j], found[1][j]).astype(B16)
                store(s.grad_qkv.at[j], g, lanes, both)

        each_pair(block, step)

    def mixed_back(k, g):
        def half(pair):
            value = nn(pair_rows(k, pair), weights[g, 3])
            s.grad_mixed[pl.ds(pair * 2, 2)] = as_flat(value.astype(B16))

        spread_near(k)
        half(y)
        spread_pass(k)
        spread_far(k)
        half(1 - y)

    def slot_grad(slot, k, b_ref):
        value = tn(gathered[k].reshape(nf * rows, width), b_ref[...].reshape(nf * rows, hidden))
        s.product[...] = value.reshape(outer, 2, part, hidden)
        s.pair_out[slot] = s.product[:, 1 - i].astype(B16)
        rcopy(
            s.pair_out.at[slot],
            s.pair_in.at[slot],
            s.pair_gs.at[slot],
            s.pair_gr.at[slot],
            mate,
        ).start()
        s.own_sum[slot] = s.product[:, i].astype(B16)

    def slot_pass(slot):
        block = s.pair_in.at[slot]
        cp = rcopy(block, block, s.pair_gs.at[slot], s.pair_gr.at[slot], mate)
        cp.wait_recv()
        cp.wait_send()

        def both(owner):
            return s.own_sum[slot, owner].astype(F32) + s.pair_in[slot, owner].astype(F32)

        def go(q):
            to = (o + q) % outer
            s.pair_out[slot, q] = both(to).astype(B16)
            rcopy(
                s.pair_out.at[slot, q],
                s.line_in.at[slot, q],
                s.line_gs.at[slot],
                s.line_gr.at[slot],
                at(to * 2 + i, f),
            ).start()

        each(1, outer, go)
        gout[slot] = both(o)

    def slot_end(slot):
        block = s.line_in.at[slot, pl.ds(1, outer - 1)]
        cp = rcopy(block, block, s.line_gs.at[slot], s.line_gr.at[slot], mate)
        cp.wait_recv()
        cp.wait_send()
        total = gout[slot]
        if outer <= 8:
            for q in range(1, outer):
                total = total + s.line_in[slot, q].astype(F32)
        else:
            total = lax.fori_loop(
                1, outer, lambda q, t: t + s.line_in[slot, q].astype(F32), total
            )
        gout[slot] = total
        folded = jnp.sum((total * total).reshape(part // 8, 8, hidden), axis=0)
        for k in range(hidden // LANES):
            s.sq_mine[0] += folded[:, k * LANES : (k + 1) * LANES]

    gather_start(0)
    hear(0, s.tiles, DP)
    s.tiles[d] = vec[...]
    per_tile = LANES // part
    for k in range(width // LANES):
        gains[:, k * LANES : (k + 1) * LANES] = total_of(
            s.tiles.at[pl.ds(k * per_tile, per_tile)], per_tile
        )
    s.vec_acc[...] = jnp.zeros_like(s.vec_acc)
    s.sq_mine[...] = jnp.zeros_like(s.sq_mine)

    def masked_rows(block):
        return jnp.broadcast_to(msk[block, :], (CHUNK, width)) > 0.5

    def first_norm(block, k):
        value = jnp.where(masked_rows(block), gains[3:4, :], tok[block, :].astype(F32))
        work[block, :] = value
        gathered[0, f, block] = norm_rows(0, value, block)

    chunks(first_norm)
    spread_start(0)
    pack(0, work)
    swap_start(0)
    gather_start(1)

    def widen(block, k):
        work[block, :] = cot[block, :].astype(F32)

    chunks(widen)
    pack(1, work)
    swap_start(1)

    spread_near(0)
    spread_pass(0)
    gather_pass(0)
    gather_start(2)
    gather_ready(0)
    project(0, 0, s.qkv.at[0], y)
    spread_far(0)
    project(0, 0, s.qkv.at[0], 1 - y)
    attention(0)
    collect_start(0, [(s.mixed.at[0], 0, 3)])
    swap_wait(1)
    gathered[1, f] = swap_in[1].reshape(rows, width)
    spread_start(1)
    gather_pass(1)
    gather_start(3)
    get = collect_end(0)

    def take_branch(block, k):
        work[block, :] = get(block)

    chunks(take_branch)
    pack(2, work)
    swap_start(2)

    swap_wait(0)
    swap_wait(2)

    def second_norm(block, k):
        value = swap_in[0, k].astype(F32) + swap_in[2, k].astype(F32)
        mid[block, :] = value
        gathered[2, f, block] = norm_rows(1, value, block)

    chunks(second_norm)
    spread_start(2)
    gather_ready(1)
    spread_near(2)
    project(2, 1, s.qkv.at[1], y)
    spread_pass(2)
    spread_far(2)
    project(2, 1, s.qkv.at[1], 1 - y)
    attention(1)
    collect_start(1, [(s.mixed.at[1], 1, 3)])
    gather_pass(2)
    spread_near(1)
    spread_pass(1)
    get = collect_end(1)

    def third_norm(block, k):
        value = mid[block, :] + get(block)
        mid[block, :] = value
        gathered[3, f, block] = norm_rows(2, value, block)

    chunks(third_norm)
    spread_start(3)

    gather_pass(3)
    gather_ready(2)
    gather_ready(3)

    def up(pair):
        def step(n):
            u = nn(pair_rows(3, pair), weights[2 + n // 2, n % 2])
            t = jnp.tanh(GELU_A * (u + GELU_B * u * u * u))
            half = 0.5 * (1.0 + t)
            s.act[n, pl.ds(pair * 2, 2)] = as_flat((u * half).astype(B16))
            bend = GELU_A * (1.0 + 3.0 * GELU_B * u * u)
            s.slope[n, pl.ds(pair * 2, 2)] = as_flat(half + 0.5 * u * (1.0 - t * t) * bend)

        loop(0, 4, step)

    spread_near(3)
    up(y)
    spread_pass(3)
    spread_far(3)
    up(1 - y)
    collect_start(2, [(s.act.at[n], 2 + n // 2, 2 + n % 2) for n in range(4)])

    spread_far(1)

    def down(pair):
        def step(n):
            grad = nn(pair_rows(1, pair), weights[2 + n // 2, 2 + n % 2])
            slope = s.slope[n, pl.ds(pair * 2, 2)].reshape(2 * rows, hidden)
            s.grad_pre[n, pl.ds(pair * 2, 2)] = as_flat((grad * slope).astype(B16))

        loop(0, 4, step)

    down(y)
    down(1 - y)
    get = collect_end(2)

    def take_output(block, k):
        swap_out[3, k] = (mid[block, :] + get(block)).astype(B16)

    chunks(take_output)
    swap_start(3)
    collect_start(3, [(s.grad_pre.at[n], 2 + n // 2, n % 2) for n in range(4)])

    def grad_up(n):
        slot_grad(8 + 4 * (n // 2) + n % 2, 3, s.grad_pre.at[n])

    def grad_down(n):
        slot_grad(10 + 4 * (n // 2) + n % 2, 1, s.act.at[n])

    loop(0, 2, grad_up)
    loop(0, 2, grad_down)
    get = collect_end(3)

    def third_back(block, k):
        value = swap_in[1, k].astype(F32) + norm_back(2, get(block), block)
        mid[block, :] = value
        gathered[4, f, block] = value.astype(B16)

    chunks(third_back)
    spread_start(4)
    loop(2, 4, grad_up)
    loop(2, 4, grad_down)

    mixed_back(4, 1)
    loop(8, 10, slot_pass)
    attention_back(1)
    collect_start(4, [(s.grad_qkv.at[j], 1, j) for j in range(3)])
    loop(0, 3, lambda j: slot_grad(4 + j, 2, s.grad_qkv.at[j]))
    slot_grad(7, 4, s.mixed.at[1])
    loop(10, 12, slot_pass)
    get = collect_end(4)

    def second_back(block, k):
        swap_out[4, k] = (mid[block, :] + norm_back(1, get(block), block)).astype(B16)

    chunks(second_back)
    swap_start(4)
    loop(12, 14, slot_pass)

    swap_wait(4)
    unpack(4, work)

    def take_carry(block, k):
        gathered[5, f, block] = work[block, :].astype(B16)

    chunks(take_carry)
    spread_start(5)
    loop(14, 16, slot_pass)
    mixed_back(5, 0)
    attention_back(0)
    collect_start(5, [(s.grad_qkv.at[j], 0, j) for j in range(3)])
    loop(0, 3, lambda j: slot_grad(j, 0, s.grad_qkv.at[j]))
    slot_grad(3, 5, s.mixed.at[0])
    loop(4, 8, slot_pass)
    get = collect_end(5)

    def first_back(block, k):
        value = work[block, :] + norm_back(0, get(block), block)
        masked = masked_rows(block)
        tgr[block, :] = jnp.where(masked, 0.0, value).astype(B16)
        s.vec_acc[3:4, :] += jnp.sum(jnp.where(masked, value, 0.0), axis=0, keepdims=True)

    chunks(first_back)

    for k in range(width // LANES):
        s.vec_out[k] = s.vec_acc[:, k * LANES : (k + 1) * LANES]
    tell(1, lambda to: s.vec_out.at[(to * part) // LANES], s.vec_in, DP)
    s.vec_in[d] = s.vec_out[(d * part) // LANES]
    swap_wait(3)
    unpack(3, mid)

    def give_output(block, k):
        out[block, :] = mid[block, :].astype(B16)

    chunks(give_output)
    loop(8, 16, slot_end)
    hear(1, s.vec_in, DP)
    s.vec_mine[...] = total_of(s.vec_in, nd)
    tell(2, lambda to: s.vec_mine, s.vec_side, TP)
    s.vec_side[f] = s.vec_mine[...]
    loop(0, 4, slot_pass)
    hear(2, s.vec_side, TP)
    grad_vec = total_of(s.vec_side, nf)
    gvec[...] = grad_vec
    loop(4, 8, slot_end)
    loop(0, 4, slot_end)

    lane = lax.broadcasted_iota(jnp.int32, (8, LANES), 1)
    first_lane = (d * part) % LANES
    owned = (lane >= first_lane) & (lane < first_lane + part)
    s.sq_mine[0] += jnp.where(owned, grad_vec * grad_vec, 0.0) * (1.0 / nf)
    tell(3, lambda to: s.sq_mine.at[0], s.sq_side, TP)
    s.sq_side[f] = s.sq_mine[0]
    hear(3, s.sq_side, TP)
    s.sq_mine[1] = total_of(s.sq_side, nf)
    tell(4, lambda to: s.sq_mine.at[1], s.sq_all, DP)
    s.sq_all[d] = s.sq_mine[1]
    for g in range(4):
        gather_end(g)
    for k in range(6):
        spread_end(k)
    for k in range(5):
        swap_end(k)
    hear(4, s.sq_all, DP)
    total = jnp.sum(total_of(s.sq_all, nd), keepdims=True)
    nrm[...] = jnp.broadcast_to(jnp.sqrt(total), (8, LANES))


def adamw_step(weight, first, second, grad, rate):
    first = BETA_FIRST * first + (1.0 - BETA_FIRST) * grad
    second = BETA_SECOND * second + (1.0 - BETA_SECOND) * grad * grad
    fix_first = 1.0 - BETA_FIRST**STEP
    fix_second = 1.0 - BETA_SECOND**STEP
    update = first / fix_first / (jnp.sqrt(second / fix_second) + ADAM_EPS)
    return (weight - rate * (update + DECAY_RATE * weight), first, second)


def local(tokens, masks, cotangent, w_in, w_out, vectors, m_in, m_out, m_vec, v_in, v_out, v_vec):
    frames, here, width = tokens.shape
    part, _, hidden = w_in.shape
    nd, nf = lax.axis_size(DP), lax.axis_size(TP)
    z = SimpleNamespace(
        rows=frames * here,
        width=width,
        hidden=hidden,
        span=FRAMES // frames,
        nd=nd,
        nf=nf,
        part=part,
        heads=hidden // HDIM,
        frames=frames,
        here=here,
    )
    rows = frames * here
    lane0 = (lax.axis_index(DP) * part) % LANES

    into = w_in.transpose(1, 0, 2).astype(B16)
    outof = w_out.transpose(0, 2, 1).astype(B16)
    shard = jnp.concatenate(
        [into[0:3], outof[0:1], into[3:6], outof[1:2], into[6:8], outof[2:4], into[8:10], outof[4:6]]
    ).reshape(4, 4, part, hidden)
    vec = lax.dynamic_update_slice(
        jnp.zeros((8, LANES), F32), vectors.astype(B16).astype(F32), (0, lane0)
    )
    scratch = scratch_of(z)
    in_vmem = pl.BlockSpec(memory_space=pltpu.VMEM)
    output, token_grad, norm, grads, grad_vec = pl.pallas_call(
        functools.partial(layer, z, list(scratch)),
        out_shape=(
            jax.ShapeDtypeStruct((rows, width), B16),
            jax.ShapeDtypeStruct((rows, width), B16),
            jax.ShapeDtypeStruct((8, LANES), F32),
            jax.ShapeDtypeStruct((16, part, hidden), F32),
            jax.ShapeDtypeStruct((8, LANES), F32),
        ),
        in_specs=[in_vmem] * 5,
        out_specs=[in_vmem] * 5,
        scratch_shapes=list(scratch.values()),
        compiler_params=pltpu.CompilerParams(
            collective_id=0, has_side_effects=True, vmem_limit_bytes=VMEM_BYTES
        ),
    )(
        tokens.reshape(rows, width),
        masks.reshape(rows, 1).astype(F32),
        cotangent.reshape(rows, width),
        shard,
        vec,
    )
    grad_norm = norm[0, 0]
    factor = CLIP_AT / jnp.maximum(grad_norm, CLIP_AT)
    grad_in = jnp.concatenate([grads[0:3], grads[4:7], grads[8:10], grads[12:14]]).transpose(1, 0, 2)
    grad_out = jnp.concatenate([grads[3:4], grads[7:8], grads[10:12], grads[14:16]]).transpose(
        0, 2, 1
    )
    grad_vec = lax.dynamic_slice(grad_vec, (0, lane0), (4, part))
    new_w_in, new_m_in, new_v_in = adamw_step(w_in, m_in, v_in, grad_in * factor, RATE_INPUT)
    new_w_out, new_m_out, new_v_out = adamw_step(
        w_out, m_out, v_out, grad_out * factor, RATE_OUTPUT
    )
    new_vectors, new_m_vec, new_v_vec = adamw_step(
        vectors, m_vec, v_vec, grad_vec * factor, RATE_VECTOR
    )
    return (
        output.reshape(frames, here, width),
        token_grad.reshape(frames, here, width),
        grad_norm,
        new_w_in,
        new_w_out,
        new_vectors,
        new_m_in,
        new_m_out,
        new_m_vec,
        new_v_in,
        new_v_out,
        new_v_vec,
    )


def solution(mesh):
    in_specs = (
        P(DP, TP, None),
        P(DP, TP),
        P(DP, TP, None),
        P(DP, None, TP),
        P(None, TP, DP),
        P(None, DP),
        P(DP, None, TP),
        P(None, TP, DP),
        P(None, DP),
        P(DP, None, TP),
        P(None, TP, DP),
        P(None, DP),
    )
    out_specs = (P(DP, TP, None), P(DP, TP, None), P()) + in_specs[3:]
    return jax.shard_map(local, mesh=mesh, in_specs=in_specs, out_specs=out_specs, check_vma=False)
```

time: 1250 us -> 370 us (0.30)
  waiting for transfers between devices: 859 us -> 0 us
  Pallas kernels: 0 us -> 339 us
  local copies, waits for them, and re-layouts: 112 us -> 20.5 us
  matrix products: 86.9 us -> 0 us
  blocking collectives: 67.3 us -> 0 us
  other arithmetic: 64.7 us -> 8.84 us
  starting transfers between devices: 30.4 us -> 0 us
  between operations: 18.9 us -> 1.49 us
    reduce_scatter x8 -> x0, waiting for transfers between devices: 466 us -> none  [the longest x1 180 us: local(): lax.psum_scatter(grad_in_full, 'dp', scatter_dimension=0, tiled=True)]
    pallas_call x0 -> x1, Pallas kernels: none -> 339 us  [local(): pl.pallas_call(functools.partial(layer, z, list(scratch)), out_shape=(jax...]
    all_gather x8 -> x0, waiting for transfers between devices: 238 us -> none  [the longest x1 89.9 us: local(): lax.all_gather(w_in.astype(b16), 'dp', axis=0, tiled=True)]
    ppermute x14 -> x0, waiting for transfers between devices: 118 us -> none  [from_behind(): lax.ppermute(value, axis, [(source, source + steps) for source in range(f...]
    dot_general x29 -> x0, matrix products: 84.7 us -> none  [the longest x1 5.58 us: local(): jnp.einsum('fshe,gshe->hfgs', grad_mixed_two, pair_all[1], preferred_elem...]
    psum x2 -> x0, blocking collectives: 45 us -> none  [the longest x1 39.4 us: local(): grad_norm = jnp.sqrt(lax.psum(local_squares, ('dp', 'fsdp')))]
    concatenate x1, local copies, waits for them, and re-layouts: 37.3 us -> 0.67 us  [local(): jnp.concatenate([into[0:3], outof[0:1], into[3:6], outof[1:2], into[6:8],...]
    unnamed x18 -> x0, waiting for transfers between devices: 36.4 us -> none
  transfers between devices with their start and end apart: 31 -> 0, of which waited for: 26 -> 0; matrix products, arithmetic and copies ran while one was open for 7% -> 0% of each run, Pallas kernels for 0% -> 0%
where the time goes in v1:
time: 370 us; the launch traced here: 369 us
  Pallas kernels  339 us (92%)
  local copies, waits for them, and re-layouts  20.5 us (6%)
  other arithmetic  8.84 us (2%)
    pallas_call x1, Pallas kernels, local(): pl.pallas_call(functools.partial(layer, z, list(scratch)), out_shape=(jax...  339 us
    unnamed x43, local copies, waits for them, and re-layouts  12.3 us

profile of v1, /device:TPU:0, one launch (start us, length us, event | category | flops | bytes accessed | tf_op | source)
XLA Modules:
  0.0 369.4 jit_solution(9415612913873768510)
XLA Ops:
  0.7 1.5 convert_bitcast_fusion
  2.1 0.7 slice_dynamic-update-slice_fusion.1
  3.0 0.6 constant_dynamic-update-slice_fusion.3
  3.6 0.7 slice_dynamic-update-slice_fusion
  4.5 0.6 constant_dynamic-update-slice_fusion.2
  5.1 0.7 slice_dynamic-update-slice_fusion.3
  5.9 0.7 constant_dynamic-update-slice_fusion.1
  6.6 0.7 slice_dynamic-update-slice_fusion.2
  7.4 0.7 constant_dynamic-update-slice_fusion
  8.0 0.8 convert_element_type.28.refs_1_
  9.4 338.5 %shard_map.211 = (bf16[128,1024]{1,0:T(8,128)(2,1)}, bf16[128,1024]{1,0:T(8,128)(2,1)}, f32[8,128]{1,0:T(8,128)}, f32[16,128,256]{2,1,0:T(8,128)}, f32[8,128]{1,0:T(8,128)}) custom-call(bf16[128,1024]{1,0:T(8,128)(2,1)} %bitcast.26, f32[128,1]{1,0:T(8,128)} %convert_element_type.28.refs_1_, bf16[128,1024]{1,0:T(8,128)(2,1)} %bitcast.27, ...), custom_call_target="tpu_custom_call" | custom-call | tf_op jit(solution)/shard_map/pallas_call | solution.py:800
  348.0 2.2 fusion.9
  350.1 1.7 fusion.8
  351.8 1.2 slice.60
  354.0 1.1 copy.30
  355.1 1.1 copy.32
  356.3 2.1 multiply_subtract_fusion.1
  358.4 1.1 copy.33
  359.6 1.1 copy.34
  360.7 1.1 copy.35
  361.9 1.2 fusion.10
  363.3 4.0 %multiply_subtract_fusion = (f32[128,10,256]{2,0,1:T(8,128)}, f32[128,10,256]{2,0,1:T(8,128)}, f32[128,10,256]{2,0,1:T(8,128)}) fusion(f32[128,10,256]{2,0,1:T(8,128)S(1)} %copy-done, f32[]{:T(128)S(6)} %div.48, f32[2,128,256]{2,1,0:T(8,128)S(1)} %copy-done.3, f32[2,128,256]{2,1,0:T(8,128)S(1)} %copy-done.4, f32[3,128,256]{2,1,0:T(8,128)S(1)} %get-tuple-element.50, ...), kind=kLoop, calls=%fused_computation.4 | loop fusion | flops 6225920 | bytes 9175044 | tf_op jit(solution)/shard_map/sub | solution.py:768
  368.0 0.7 copy.45
  368.7 0.7 copy.46
  (40 shorter events, 2.2 us)
Async XLA Ops:
  0.6 2.2 copy-start.1
  3.6 4.4 %copy-start.12 = (s32[2,64]{1,0:T(2,128)S(1)}, s32[2,64]{1,0:T(2,128)}, u32[]{:S(2)}) copy-start(s32[2,64]{1,0:T(2,128)} %param.13) | copy-start | bytes 1540
  4.3 4.5 %copy-start.9 = (f32[4,128]{1,0:T(4,128)S(1)}, f32[4,128]{1,0:T(4,128)}, u32[]{:S(2)}) copy-start(f32[4,128]{1,0:T(4,128)} %param.17) | copy-start | bytes 6148
  347.9 5.8 %copy-start.5 = (f32[6,256,128]{2,1,0:T(8,128)S(1)}, f32[6,256,128]{2,1,0:T(8,128)}, u32[]{:S(2)}) copy-start(f32[6,256,128]{2,1,0:T(8,128)} %param.19) | copy-start | bytes 2359300
  350.1 3.9 %copy-start.6 = (f32[6,256,128]{2,1,0:T(8,128)S(1)}, f32[6,256,128]{2,1,0:T(8,128)}, u32[]{:S(2)}) copy-start(f32[6,256,128]{2,1,0:T(8,128)} %param.22) | copy-start | bytes 2359300
  360.7 2.4 copy-start
  360.7 2.4 copy-start.2
  361.9 1.4 copy-start.3
  361.9 1.5 copy-start.4
  363.3 4.0 %copy-start.10 = (f32[4,128]{1,0:T(4,128)S(1)}, f32[4,128]{1,0:T(4,128)}, u32[]{:S(2)}) copy-start(f32[4,128]{1,0:T(4,128)} %param.20) | copy-start | bytes 6148
  363.3 4.0 %copy-start.11 = (f32[4,128]{1,0:T(4,128)S(1)}, f32[4,128]{1,0:T(4,128)}, u32[]{:S(2)}) copy-start(f32[4,128]{1,0:T(4,128)} %param.23) | copy-start | bytes 6148
  363.3 4.0 %copy-start.13 = (f32[8,128]{1,0:T(8,128)S(1)}, f32[8,128]{1,0:T(8,128)}, u32[]{:S(2)}) copy-start(f32[8,128]{1,0:T(8,128)} %get-tuple-element.21) | copy-start | bytes 12292
  363.3 4.6 %copy-start.8 = (bf16[128,1024]{1,0:T(8,128)(2,1)S(1)}, bf16[128,1024]{1,0:T(8,128)(2,1)}, u32[]{:S(2)}) copy-start(bf16[128,1024]{1,0:T(8,128)(2,1)} %get-tuple-element.17) | copy-start | bytes 786436
  363.3 5.3 %copy-start.7 = (bf16[128,1024]{1,0:T(8,128)(2,1)S(1)}, bf16[128,1024]{1,0:T(8,128)(2,1)}, u32[]{:S(2)}) copy-start(bf16[128,1024]{1,0:T(8,128)(2,1)} %get-tuple-element.18) | copy-start | bytes 786436

commit v2 on v1

--- a/solution.py
+++ b/solution.py
@@ -76,6 +76,10 @@
     vmem = pltpu.VMEM
     dma = pltpu.SemaphoreType.DMA
     return dict(
+        stage_in=vmem((10, part, hidden), F32),
+        stage_out=vmem((6, hidden, part), F32),
+        shard=vmem((4, 4, part, hidden), B16),
+        tile=vmem((8, LANES), F32),
         weights=vmem((4, 4, width, hidden), B16),
         gathered=vmem((6, nf, rows, width), B16),
         gains=vmem((8, width), F32),
@@ -84,8 +88,8 @@
         rstds=vmem((3, rows, LANES), F32),
         work=vmem((rows, width), F32),
         mid=vmem((rows, width), F32),
-        swap_out=vmem((5, span, CHUNK, width), B16),
-        swap_in=vmem((5, span, CHUNK, width), B16),
+        swap_out=vmem((4, span, CHUNK, width), B16),
+        swap_in=vmem((4, span, CHUNK, width), B16),
         part_sum=vmem((2, 2, rows, width), F32),
         sib_out=vmem((2, 2, rows, width), B16),
         sib_in=vmem((2, 2, rows, width), B16),
@@ -124,8 +128,9 @@
         row_r=dma((6, 3)),
         sum_s=dma((6, 3)),
         sum_r=dma((6, 3)),
-        swap_s=dma((5,)),
-        swap_r=dma((5,)),
+        swap_s=dma((4,)),
+        swap_r=dma((4,)),
+        stage_s=dma((16,)),
         pair_gs=dma((16,)),
         pair_gr=dma((16,)),
         line_gs=dma((16,)),
@@ -134,9 +139,9 @@
 
 
 def layer(z, names, *refs):
-    tok, msk, cot, shard, vec = refs[:5]
-    out, tgr, nrm, gout, gvec = refs[5:10]
-    s = SimpleNamespace(**dict(zip(names, refs[10:])))
+    tok, msk, cot, w_in, w_out, vec = refs[:6]
+    out, tgr, nrm, gout, gvec = refs[6:11]
+    s = SimpleNamespace(**dict(zip(names, refs[11:])))
     rows, width, hidden, span = z.rows, z.width, z.hidden, z.span
     nd, nf, part, heads = z.nd, z.nf, z.part, z.heads
     frames, here = z.frames, z.here
@@ -145,7 +150,7 @@
     n_pairs = heads // 2
     scale = HDIM**-0.5
     gathered, weights, gains = s.gathered, s.weights, s.gains
-    work, mid = s.work, s.mid
+    work, mid, shard = s.work, s.mid, s.shard
     swap_out, swap_in = s.swap_out, s.swap_in
 
     d, f = lax.axis_index(DP), lax.axis_index(TP)
@@ -163,6 +168,29 @@
             src_ref=src, dst_ref=dst, send_sem=ssem, recv_sem=rsem, device_id=dev, device_id_type=MESH
         )
 
+    in_slots = {0: [0, 1, 2], 1: [3, 4, 5], 2: [6, 7, 8, 9], 3: []}
+    out_slots = {0: [0], 1: [1], 2: [], 3: [2, 3, 4, 5]}
+
+    def stage(g):
+        for n in in_slots[g]:
+            yield pltpu.make_async_copy(w_in.at[n], s.stage_in.at[n], s.stage_s.at[n])
+        for n in out_slots[g]:
+            yield pltpu.make_async_copy(w_out.at[n], s.stage_out.at[n], s.stage_s.at[10 + n])
+
+    def round_group(g):
+        for cp in stage(g):
+            cp.wait()
+        for j, n in enumerate(in_slots[g]):
+            shard[g, j] = s.stage_in[n].astype(B16)
+        for j, n in enumerate(out_slots[g]):
+            shard[g, len(in_slots[g]) + j] = s.stage_out[n].T.astype(B16)
+
+    for g in range(4):
+        for cp in stage(g):
+            cp.start()
+    s.tile[...] = jnp.zeros_like(s.tile)
+    s.tile[0:4, :] = vec[...].astype(B16).astype(F32)
+
     bar = pltpu.get_barrier_semaphore()
 
     def greet(q):
@@ -200,29 +228,32 @@
             return total
         return lax.fori_loop(1, count, lambda k, t: t + ref[k], total)
 
-    tell(0, lambda to: vec, s.tiles, DP)
+    tell(0, lambda to: s.tile, s.tiles, DP)
 
     def shard_rows(owner):
         return pl.ds(pl.multiple_of(owner * part, part), part)
 
-    def gather_start(g):
+    def gather_own(g):
         mine = weights.at[g, :, shard_rows(d), :]
         pltpu.make_async_copy(shard.at[g], mine, s.copy_w.at[g]).start()
+        rcopy(shard.at[g], mine, s.pair_ws.at[g], s.pair_wr.at[g], mate).start()
+
+    def gather_line(g, low, high):
+        mine = weights.at[g, :, shard_rows(d), :]
 
         def go(q):
             dev = at(((o + q) % outer) * 2 + i, f)
             rcopy(shard.at[g], mine, s.line_ws.at[g], s.line_wr.at[g, q], dev).start()
 
-        each(1, outer, go)
-        rcopy(shard.at[g], mine, s.pair_ws.at[g], s.pair_wr.at[g], mate).start()
-
-    def gather_pass(g):
+        each(low, high, go)
+
+    def gather_pass(g, low, high):
         def go(q):
             block = weights.at[g, :, shard_rows(((o + outer - q) % outer) * 2 + i), :]
             rcopy(block, block, s.line_ws.at[g], s.line_wr.at[g, q], mate).wait_recv()
             rcopy(block, block, s.pair_ws.at[g], s.pair_wr.at[g], mate).start()
 
-        each(1, outer, go)
+        each(low, high, go)
 
     def gather_ready(g):
         mine = weights.at[g, :, shard_rows(d), :]
@@ -470,10 +501,13 @@
         spread_far(k)
         half(1 - y)
 
-    def slot_grad(slot, k, b_ref):
+    def slot_make(slot, k, b_ref):
         value = tn(gathered[k].reshape(nf * rows, width), b_ref[...].reshape(nf * rows, hidden))
         s.product[...] = value.reshape(outer, 2, part, hidden)
         s.pair_out[slot] = s.product[:, 1 - i].astype(B16)
+        s.own_sum[slot] = s.product[:, i].astype(B16)
+
+    def slot_send(slot):
         rcopy(
             s.pair_out.at[slot],
             s.pair_in.at[slot],
@@ -481,7 +515,6 @@
             s.pair_gr.at[slot],
             mate,
         ).start()
-        s.own_sum[slot] = s.product[:, i].astype(B16)
 
     def slot_pass(slot):
         block = s.pair_in.at[slot]
@@ -524,9 +557,11 @@
         for k in range(hidden // LANES):
             s.sq_mine[0] += folded[:, k * LANES : (k + 1) * LANES]
 
-    gather_start(0)
+    round_group(0)
+    gather_line(0, 1, outer)
+    gather_own(0)
     hear(0, s.tiles, DP)
-    s.tiles[d] = vec[...]
+    s.tiles[d] = s.tile[...]
     per_tile = LANES // part
     for k in range(width // LANES):
         gains[:, k * LANES : (k + 1) * LANES] = total_of(
@@ -545,62 +580,73 @@
 
     chunks(first_norm)
     spread_start(0)
-    pack(0, work)
+    round_group(1)
+    gather_line(1, 1, outer)
+    gather_pass(0, 1, 2)
+
+    def widen(block, k):
+        s.part_sum[0, 0, block, :] = cot[block, :].astype(F32)
+
+    chunks(widen)
+    pack(0, s.part_sum.at[0, 0])
     swap_start(0)
-    gather_start(1)
-
-    def widen(block, k):
-        work[block, :] = cot[block, :].astype(F32)
-
-    chunks(widen)
-    pack(1, work)
-    swap_start(1)
-
+
+    gather_pass(0, 2, outer - 1)
     spread_near(0)
     spread_pass(0)
-    gather_pass(0)
-    gather_start(2)
+    gather_pass(0, outer - 1, outer)
+    gather_own(1)
+    round_group(2)
+    gather_line(2, 1, 2)
     gather_ready(0)
     project(0, 0, s.qkv.at[0], y)
     spread_far(0)
     project(0, 0, s.qkv.at[0], 1 - y)
+    gather_pass(1, 1, 2)
     attention(0)
+    gather_pass(1, 2, outer - 1)
     collect_start(0, [(s.mixed.at[0], 0, 3)])
+    gather_pass(1, outer - 1, outer)
+    round_group(3)
+    get = collect_end(0)
+
+    def take_branch(block, k):
+        work[block, :] = work[block, :] + get(block)
+
+    chunks(take_branch)
+    pack(1, work)
+    swap_start(1)
+    gather_line(2, 2, outer)
+    gather_line(3, 1, outer)
+    gather_own(2)
+
+    swap_wait(0)
+    gathered[1, f] = swap_in[0].reshape(rows, width)
+    spread_start(1)
+    gather_pass(2, 1, 2)
+    gather_own(3)
     swap_wait(1)
-    gathered[1, f] = swap_in[1].reshape(rows, width)
-    spread_start(1)
-    gather_pass(1)
-    gather_start(3)
-    get = collect_end(0)
-
-    def take_branch(block, k):
-        work[block, :] = get(block)
-
-    chunks(take_branch)
-    pack(2, work)
-    swap_start(2)
-
-    swap_wait(0)
-    swap_wait(2)
 
     def second_norm(block, k):
-        value = swap_in[0, k].astype(F32) + swap_in[2, k].astype(F32)
+        value = swap_in[1, k].astype(F32)
         mid[block, :] = value
         gathered[2, f, block] = norm_rows(1, value, block)
 
     chunks(second_norm)
     spread_start(2)
+    spread_near(1)
+    spread_pass(1)
     gather_ready(1)
     spread_near(2)
     project(2, 1, s.qkv.at[1], y)
     spread_pass(2)
     spread_far(2)
     project(2, 1, s.qkv.at[1], 1 - y)
+    gather_pass(2, 2, outer - 1)
     attention(1)
+    gather_pass(2, outer - 1, outer)
     collect_start(1, [(s.mixed.at[1], 1, 3)])
-    gather_pass(2)
-    spread_near(1)
-    spread_pass(1)
+    gather_pass(3, 1, 2)
     get = collect_end(1)
 
     def third_norm(block, k):
@@ -610,14 +656,13 @@
 
     chunks(third_norm)
     spread_start(3)
-
-    gather_pass(3)
-    gather_ready(2)
-    gather_ready(3)
+    spread_far(1)
+    gather_pass(3, 2, outer - 1)
+
 
     def up(pair):
         def step(n):
-            u = nn(pair_rows(3, pair), weights[2 + n // 2, n % 2])
+            u = nn(pair_rows(3, pair), weights[2, n])
             t = jnp.tanh(GELU_A * (u + GELU_B * u * u * u))
             half = 0.5 * (1.0 + t)
             s.act[n, pl.ds(pair * 2, 2)] = as_flat((u * half).astype(B16))
@@ -626,85 +671,104 @@
 
         loop(0, 4, step)
 
+    def down(pair):
+        def step(n):
+            grad = nn(pair_rows(1, pair), weights[3, n])
+            slope = s.slope[n, pl.ds(pair * 2, 2)].reshape(2 * rows, hidden)
+            s.grad_pre[n, pl.ds(pair * 2, 2)] = as_flat((grad * slope).astype(B16))
+
+        loop(0, 4, step)
+
+    gather_ready(2)
     spread_near(3)
     up(y)
     spread_pass(3)
+    gather_pass(3, outer - 1, outer)
     spread_far(3)
     up(1 - y)
-    collect_start(2, [(s.act.at[n], 2 + n // 2, 2 + n % 2) for n in range(4)])
-
-    spread_far(1)
-
-    def down(pair):
-        def step(n):
-            grad = nn(pair_rows(1, pair), weights[2 + n // 2, 2 + n % 2])
-            slope = s.slope[n, pl.ds(pair * 2, 2)].reshape(2 * rows, hidden)
-            s.grad_pre[n, pl.ds(pair * 2, 2)] = as_flat((grad * slope).astype(B16))
-
-        loop(0, 4, step)
-
+    loop(0, 4, lambda n: slot_make(12 + n, 1, s.act.at[n]))
+    slot_send(12)
+    slot_send(13)
+    gather_ready(3)
+
+    down(1 - y)
     down(y)
-    down(1 - y)
+    slot_make(8, 3, s.grad_pre.at[0])
+    slot_send(8)
+    collect_start(2, [(s.grad_pre.at[n], 2, n) for n in range(4)])
+    slot_pass(12)
+    loop(1, 4, lambda n: slot_make(8 + n, 3, s.grad_pre.at[n]))
+    slot_send(9)
+    slot_send(14)
+    slot_pass(13)
     get = collect_end(2)
 
-    def take_output(block, k):
-        swap_out[3, k] = (mid[block, :] + get(block)).astype(B16)
-
-    chunks(take_output)
-    swap_start(3)
-    collect_start(3, [(s.grad_pre.at[n], 2 + n // 2, n % 2) for n in range(4)])
-
-    def grad_up(n):
-        slot_grad(8 + 4 * (n // 2) + n % 2, 3, s.grad_pre.at[n])
-
-    def grad_down(n):
-        slot_grad(10 + 4 * (n // 2) + n % 2, 1, s.act.at[n])
-
-    loop(0, 2, grad_up)
-    loop(0, 2, grad_down)
-    get = collect_end(3)
-
     def third_back(block, k):
-        value = swap_in[1, k].astype(F32) + norm_back(2, get(block), block)
-        mid[block, :] = value
+        value = swap_in[0, k].astype(F32) + norm_back(2, get(block), block)
+        work[block, :] = value
         gathered[4, f, block] = value.astype(B16)
 
     chunks(third_back)
     spread_start(4)
-    loop(2, 4, grad_up)
-    loop(2, 4, grad_down)
+    slot_pass(8)
+    slot_send(10)
+    slot_send(15)
+    collect_start(3, [(s.act.at[n], 3, n) for n in range(4)])
+    slot_pass(9)
 
     mixed_back(4, 1)
-    loop(8, 10, slot_pass)
+    slot_make(7, 4, s.mixed.at[1])
+    slot_pass(14)
+    slot_send(11)
+    slot_send(7)
+    get_output = collect_end(3)
+
+    def take_output(block, k):
+        swap_out[2, k] = (mid[block, :] + get_output(block)).astype(B16)
+
+    chunks(take_output)
+    swap_start(2)
     attention_back(1)
+    slot_pass(10)
     collect_start(4, [(s.grad_qkv.at[j], 1, j) for j in range(3)])
-    loop(0, 3, lambda j: slot_grad(4 + j, 2, s.grad_qkv.at[j]))
-    slot_grad(7, 4, s.mixed.at[1])
-    loop(10, 12, slot_pass)
+    slot_pass(15)
+    loop(0, 3, lambda j: slot_make(4 + j, 2, s.grad_qkv.at[j]))
+    slot_pass(11)
     get = collect_end(4)
 
     def second_back(block, k):
-        swap_out[4, k] = (mid[block, :] + norm_back(1, get(block), block)).astype(B16)
+        swap_out[3, k] = (work[block, :] + norm_back(1, get(block), block)).astype(B16)
 
     chunks(second_back)
-    swap_start(4)
-    loop(12, 14, slot_pass)
-
-    swap_wait(4)
-    unpack(4, work)
+    swap_start(3)
+    slot_send(4)
+    slot_send(5)
+    slot_send(6)
+
+    swap_wait(3)
+    unpack(3, work)
 
     def take_carry(block, k):
         gathered[5, f, block] = work[block, :].astype(B16)
 
     chunks(take_carry)
     spread_start(5)
-    loop(14, 16, slot_pass)
+    slot_pass(7)
     mixed_back(5, 0)
+    slot_make(3, 5, s.mixed.at[0])
+    slot_send(3)
+    slot_pass(4)
     attention_back(0)
+
+    def spatial_slot(j):
+        slot_make(j, 0, s.grad_qkv.at[j])
+        slot_send(j)
+
+    loop(0, 3, spatial_slot)
+    slot_pass(5)
     collect_start(5, [(s.grad_qkv.at[j], 0, j) for j in range(3)])
-    loop(0, 3, lambda j: slot_grad(j, 0, s.grad_qkv.at[j]))
-    slot_grad(3, 5, s.mixed.at[0])
-    loop(4, 8, slot_pass)
+    slot_pass(6)
+    slot_pass(3)
     get = collect_end(5)
 
     def first_back(block, k):
@@ -719,24 +783,27 @@
         s.vec_out[k] = s.vec_acc[:, k * LANES : (k + 1) * LANES]
     tell(1, lambda to: s.vec_out.at[(to * part) // LANES], s.vec_in, DP)
     s.vec_in[d] = s.vec_out[(d * part) // LANES]
-    swap_wait(3)
-    unpack(3, mid)
+    slot_pass(0)
+    swap_wait(2)
+    unpack(2, mid)
 
     def give_output(block, k):
         out[block, :] = mid[block, :].astype(B16)
 
     chunks(give_output)
     loop(8, 16, slot_end)
+    slot_pass(1)
     hear(1, s.vec_in, DP)
     s.vec_mine[...] = total_of(s.vec_in, nd)
     tell(2, lambda to: s.vec_mine, s.vec_side, TP)
     s.vec_side[f] = s.vec_mine[...]
-    loop(0, 4, slot_pass)
+    loop(4, 8, slot_end)
+    slot_end(3)
+    slot_pass(2)
     hear(2, s.vec_side, TP)
     grad_vec = total_of(s.vec_side, nf)
     gvec[...] = grad_vec
-    loop(4, 8, slot_end)
-    loop(0, 4, slot_end)
+    loop(0, 3, slot_end)
 
     lane = lax.broadcasted_iota(jnp.int32, (8, LANES), 1)
     first_lane = (d * part) % LANES
@@ -752,7 +819,7 @@
         gather_end(g)
     for k in range(6):
         spread_end(k)
-    for k in range(5):
+    for k in range(4):
         swap_end(k)
     hear(4, s.sq_all, DP)
     total = jnp.sum(total_of(s.sq_all, nd), keepdims=True)
@@ -766,6 +833,43 @@
     fix_second = 1.0 - BETA_SECOND**STEP
     update = first / fix_first / (jnp.sqrt(second / fix_second) + ADAM_EPS)
     return (weight - rate * (update + DECAY_RATE * weight), first, second)
+
+
+def in_slot(j):
+    return jnp.where(j < 3, j, jnp.where(j < 6, j + 1, j + 2))
+
+
+def out_slot(j):
+    k = jnp.minimum(j, 5)
+    return jnp.where(k == 0, 3, jnp.where(k == 1, 7, k + 10))
+
+
+def updates(*refs):
+    grad_in, grad_out, grad_vec, norm, out, tgr = refs[:6]
+    state = refs[6:15]
+    new = refs[15:24]
+    new_out, new_tgr, new_norm = refs[24:]
+    j = pl.program_id(0)
+    grad_norm = norm[0:1, 0:1]
+    factor = CLIP_AT / jnp.maximum(grad_norm, CLIP_AT)
+
+    def update(n, grad, rate):
+        values = adamw_step(*(state[3 * n + k][...] for k in range(3)), grad * factor, rate)
+        for k in range(3):
+            new[3 * n + k][...] = values[k]
+
+    update(0, grad_in[...], RATE_INPUT)
+
+    @pl.when(j < 6)
+    def _():
+        update(1, grad_out[0].T[None], RATE_OUTPUT)
+
+    @pl.when(j == 9)
+    def _():
+        update(2, grad_vec[0:4, :], RATE_VECTOR)
+        new_out[...] = out[...]
+        new_tgr[...] = tgr[...]
+        new_norm[...] = grad_norm
 
 
 def local(tokens, masks, cotangent, w_in, w_out, vectors, m_in, m_out, m_vec, v_in, v_out, v_vec):
@@ -787,14 +891,18 @@
     rows = frames * here
     lane0 = (lax.axis_index(DP) * part) % LANES
 
-    into = w_in.transpose(1, 0, 2).astype(B16)
-    outof = w_out.transpose(0, 2, 1).astype(B16)
-    shard = jnp.concatenate(
-        [into[0:3], outof[0:1], into[3:6], outof[1:2], into[6:8], outof[2:4], into[8:10], outof[4:6]]
-    ).reshape(4, 4, part, hidden)
-    vec = lax.dynamic_update_slice(
-        jnp.zeros((8, LANES), F32), vectors.astype(B16).astype(F32), (0, lane0)
-    )
+    def as_tile(value):
+        if part == LANES:
+            return value
+        return lax.dynamic_update_slice(jnp.zeros((4, LANES), F32), value, (0, lane0))
+
+    def of_tile(value):
+        return value if part == LANES else lax.dynamic_slice(value, (0, lane0), (4, part))
+
+    def by_slot(value):
+        return value.transpose(1, 0, 2)
+
+    vec = as_tile(vectors)
     scratch = scratch_of(z)
     in_vmem = pl.BlockSpec(memory_space=pltpu.VMEM)
     output, token_grad, norm, grads, grad_vec = pl.pallas_call(
@@ -806,7 +914,7 @@
             jax.ShapeDtypeStruct((16, part, hidden), F32),
             jax.ShapeDtypeStruct((8, LANES), F32),
         ),
-        in_specs=[in_vmem] * 5,
+        in_specs=[in_vmem] * 3 + [pl.BlockSpec(memory_space=pl.ANY)] * 2 + [in_vmem],
         out_specs=[in_vmem] * 5,
         scratch_shapes=list(scratch.values()),
         compiler_params=pltpu.CompilerParams(
@@ -816,36 +924,60 @@
         tokens.reshape(rows, width),
         masks.reshape(rows, 1).astype(F32),
         cotangent.reshape(rows, width),
-        shard,
+        by_slot(w_in),
+        w_out,
         vec,
     )
-    grad_norm = norm[0, 0]
-    factor = CLIP_AT / jnp.maximum(grad_norm, CLIP_AT)
-    grad_in = jnp.concatenate([grads[0:3], grads[4:7], grads[8:10], grads[12:14]]).transpose(1, 0, 2)
-    grad_out = jnp.concatenate([grads[3:4], grads[7:8], grads[10:12], grads[14:16]]).transpose(
-        0, 2, 1
+
+    def whole(shape):
+        return pl.BlockSpec(shape, lambda j: (0,) * len(shape))
+
+    slot_in = pl.BlockSpec((1, part, hidden), lambda j: (j, 0, 0))
+    slot_out = pl.BlockSpec((1, hidden, part), lambda j: (jnp.minimum(j, 5), 0, 0))
+    state_specs = [slot_in] * 3 + [slot_out] * 3 + [whole((4, LANES))] * 3
+    row_specs = [whole((rows, width))] * 2
+    state = (
+        by_slot(w_in),
+        by_slot(m_in),
+        by_slot(v_in),
+        w_out,
+        m_out,
+        v_out,
+        vec,
+        as_tile(m_vec),
+        as_tile(v_vec),
     )
-    grad_vec = lax.dynamic_slice(grad_vec, (0, lane0), (4, part))
-    new_w_in, new_m_in, new_v_in = adamw_step(w_in, m_in, v_in, grad_in * factor, RATE_INPUT)
-    new_w_out, new_m_out, new_v_out = adamw_step(
-        w_out, m_out, v_out, grad_out * factor, RATE_OUTPUT
-    )
-    new_vectors, new_m_vec, new_v_vec = adamw_step(
-        vectors, m_vec, v_vec, grad_vec * factor, RATE_VECTOR
-    )
+    new = pl.pallas_call(
+        updates,
+        grid=(10,),
+        out_shape=tuple(jax.ShapeDtypeStruct(a.shape, F32) for a in state)
+        + (jax.ShapeDtypeStruct((rows, width), B16),) * 2
+        + (jax.ShapeDtypeStruct((1, 1), F32),),
+        in_specs=[
+            pl.BlockSpec((1, part, hidden), lambda j: (in_slot(j), 0, 0)),
+            pl.BlockSpec((1, part, hidden), lambda j: (out_slot(j), 0, 0)),
+            whole((8, LANES)),
+            whole((8, LANES)),
+        ]
+        + row_specs
+        + state_specs,
+        out_specs=state_specs + row_specs + [whole((1, 1))],
+    )(grads, grads, grad_vec, norm, output, token_grad, *state)
+    new_w_in, new_m_in, new_v_in, new_w_out, new_m_out, new_v_out = new[:6]
+    new_vectors, new_m_vec, new_v_vec, output, token_grad, norm = new[6:]
     return (
         output.reshape(frames, here, width),
         token_grad.reshape(frames, here, width),
-        grad_norm,
-        new_w_in,
+        norm.reshape(()),
+        by_slot(new_w_in),
         new_w_out,
-        new_vectors,
-        new_m_in,
+        of_tile(new_vectors),
+        by_slot(new_m_in),
         new_m_out,
-        new_m_vec,
-        new_v_in,
+        of_tile(new_m_vec),
+        by_slot(new_v_in),
         new_v_out,
-        new_v_vec,
+        of_tile(new_v_vec),
     )
 
 

time: 370 us -> 273 us (0.74)
  Pallas kernels: 339 us -> 271 us
  local copies, waits for them, and re-layouts: 20.5 us -> 0.77 us
  other arithmetic: 8.84 us -> 0.68 us
    pallas_call x1, Pallas kernels: 339 us -> 260 us  [local(): pl.pallas_call(functools.partial(layer, z, list(scratch)), out_shape=(jax...]
    unnamed x43 -> x0, local copies, waits for them, and re-layouts: 12.3 us -> none
    pallas_call x0 -> x1, Pallas kernels: none -> 11.2 us  [local(): pl.pallas_call(updates, grid=(10,), out_shape=tuple((jax.ShapeDtypeStruct...]
    slice x10 -> x0, local copies, waits for them, and re-layouts: 6.76 us -> none  [the longest x1 2.15 us: local(): grads[10:12]]
    sub x3 -> x0, other arithmetic: 6.71 us -> none  [adamw_step(): return (weight - rate * (update + DECAY_RATE * weight), first, second)]
where the time goes in v2:
time: 273 us
  Pallas kernels  271 us (99%)
    pallas_call x1, Pallas kernels, local(): pl.pallas_call(functools.partial(layer, z, list(scratch)), out_shape=(jax...  260 us
    pallas_call x1, Pallas kernels, local(): pl.pallas_call(updates, grid=(10,), out_shape=tuple((jax.ShapeDtypeStruct...  11.2 us

profile of v2, /device:TPU:0, one launch (start us, length us, event | category | flops | bytes accessed | tf_op | source)
XLA Modules:
  0.0 273.1 jit_solution(12467263415532832728)
XLA Ops:
  0.6 0.7 convert_element_type.5
  1.3 0.8 convert_element_type.7.refs_1_
  2.1 259.6 %shard_map.211 = (bf16[128,1024]{1,0:T(8,128)(2,1)}, bf16[128,1024]{1,0:T(8,128)(2,1)}, f32[8,128]{1,0:T(8,128)}, f32[16,128,256]{2,1,0:T(8,128)}, f32[8,128]{1,0:T(8,128)}) custom-call(bf16[128,1024]{1,0:T(8,128)(2,1)} %bitcast.15, f32[128,1]{1,0:T(8,128)} %convert_element_type.7.refs_1_, bf16[128,1024]{1,0:T(8,128)(2,1)} %bitcast.16, ...), custom_call_target="tpu_custom_call" | custom-call | tf_op jit(solution)/shard_map/pallas_call | solution.py:908
  261.7 11.2 %shard_map.212 = (f32[10,128,256]{2,1,0:T(8,128)}, f32[10,128,256]{2,1,0:T(8,128)}, f32[10,128,256]{2,1,0:T(8,128)}, f32[6,256,128]{2,1,0:T(8,128)}, f32[6,256,1...) custom-call(f32[16,128,256]{2,1,0:T(8,128)} %get-tuple-element.29.re, ...), custom_call_target="tpu_custom_call" | custom-call | tf_op jit(solution)/shard_map/pallas_call | solution.py:950

commit v3 on v2

--- a/solution.py
+++ b/solution.py
@@ -80,6 +80,7 @@
         stage_out=vmem((6, hidden, part), F32),
         shard=vmem((4, 4, part, hidden), B16),
         tile=vmem((8, LANES), F32),
+        masked=vmem((rows, LANES), F32),
         weights=vmem((4, 4, width, hidden), B16),
         gathered=vmem((6, nf, rows, width), B16),
         gains=vmem((8, width), F32),
@@ -123,6 +124,11 @@
         line_wr=dma((4, outer)),
         pair_ws=dma((4,)),
         pair_wr=dma((4,)),
+        pair_wo=dma((4,)),
+        own_ws=dma((4,)),
+        near_ws=dma((4,)),
+        near_wr=dma((4,)),
+        far_ws=dma((4,)),
         copy_w=dma((4,)),
         row_s=dma((6, 3)),
         row_r=dma((6, 3)),
@@ -140,8 +146,8 @@
 
 def layer(z, names, *refs):
     tok, msk, cot, w_in, w_out, vec = refs[:6]
-    out, tgr, nrm, gout, gvec = refs[6:11]
-    s = SimpleNamespace(**dict(zip(names, refs[11:])))
+    out, tgr, nrm, gin, gout, gvec = refs[6:12]
+    s = SimpleNamespace(**dict(zip(names, refs[12:])))
     rows, width, hidden, span = z.rows, z.width, z.hidden, z.span
     nd, nf, part, heads = z.nd, z.nf, z.part, z.heads
     frames, here = z.frames, z.here
@@ -191,6 +197,14 @@
     s.tile[...] = jnp.zeros_like(s.tile)
     s.tile[0:4, :] = vec[...].astype(B16).astype(F32)
 
+    same = lax.broadcasted_iota(jnp.int32, (here, here), 0) == lax.broadcasted_iota(
+        jnp.int32, (here, here), 1
+    )
+    for fr in range(frames):
+        line = jnp.broadcast_to(msk[fr : fr + 1, :], (here, here)).astype(F32)
+        column = jnp.sum(jnp.where(same, line, 0.0), axis=1, keepdims=True)
+        s.masked[fr * here : (fr + 1) * here, :] = jnp.broadcast_to(column, (here, LANES))
+
     bar = pltpu.get_barrier_semaphore()
 
     def greet(q):
@@ -230,42 +244,116 @@
 
     tell(0, lambda to: s.tile, s.tiles, DP)
 
+    four = outer == 4
+    near_row = o + 1 - 2 * (o % 2)
+    next_row = jnp.where(o < 2, 2, 1)
+    last_row = jnp.where(o < 2, 3, 0)
+    middle = (o == 1) | (o == 2)
+
     def shard_rows(owner):
         return pl.ds(pl.multiple_of(owner * part, part), part)
 
+    def shard_of(g, row, col):
+        return weights.at[g, :, shard_rows(row * 2 + col), :]
+
     def gather_own(g):
-        mine = weights.at[g, :, shard_rows(d), :]
+        mine = shard_of(g, o, i)
         pltpu.make_async_copy(shard.at[g], mine, s.copy_w.at[g]).start()
-        rcopy(shard.at[g], mine, s.pair_ws.at[g], s.pair_wr.at[g], mate).start()
+        rcopy(shard.at[g], mine, s.own_ws.at[g], s.pair_wo.at[g], mate).start()
 
     def gather_line(g, low, high):
-        mine = weights.at[g, :, shard_rows(d), :]
-
         def go(q):
-            dev = at(((o + q) % outer) * 2 + i, f)
-            rcopy(shard.at[g], mine, s.line_ws.at[g], s.line_wr.at[g, q], dev).start()
+            to = (o + q) % outer
+
+            def start():
+                rcopy(
+                    shard.at[g],
+                    shard_of(g, o, i),
+                    s.line_ws.at[g],
+                    s.line_wr.at[g, o],
+                    at(to * 2 + i, f),
+                ).start()
+
+            if four:
+                pl.when(jnp.abs(to - o) < 3)(start)
+            else:
+                start()
 
         each(low, high, go)
 
+    def gather_from(g, row):
+        block = shard_of(g, row, i)
+        rcopy(block, block, s.line_ws.at[g], s.line_wr.at[g, row], mate).wait_recv()
+        return block
+
     def gather_pass(g, low, high):
-        def go(q):
-            block = weights.at[g, :, shard_rows(((o + outer - q) % outer) * 2 + i), :]
-            rcopy(block, block, s.line_ws.at[g], s.line_wr.at[g, q], mate).wait_recv()
-            rcopy(block, block, s.pair_ws.at[g], s.pair_wr.at[g], mate).start()
-
-        each(low, high, go)
+        if not four:
+
+            def go(q):
+                block = gather_from(g, (o + outer - q) % outer)
+                rcopy(block, block, s.pair_ws.at[g], s.pair_wr.at[g], mate).start()
+
+            each(low, high, go)
+            return
+        for q in range(low, high):
+            if q == 1:
+                block = shard_of(g, o, 1 - i)
+                rcopy(block, block, s.pair_ws.at[g], s.pair_wo.at[g], mate).wait_recv()
+                half = block.at[pl.ds(2, 2)]
+                dev = at(near_row * 2 + i, f)
+                rcopy(half, half, s.near_ws.at[g], s.near_wr.at[g], dev).start()
+                half = gather_from(g, near_row).at[pl.ds(0, 2)]
+                rcopy(half, half, s.pair_ws.at[g], s.pair_wr.at[g], mate).start()
+            else:
+                row = next_row if q == 2 else last_row
+                block = gather_from(g, row)
+
+                @pl.when(middle & (row == last_row))
+                def _():
+                    dev = at((3 - last_row) * 2 + i, f)
+                    rcopy(block, block, s.far_ws.at[g], s.line_wr.at[g, row], dev).start()
+
+                rcopy(block, block, s.pair_ws.at[g], s.pair_wr.at[g], mate).start()
 
     def gather_ready(g):
-        mine = weights.at[g, :, shard_rows(d), :]
+        mine = shard_of(g, o, i)
         pltpu.make_async_copy(shard.at[g], mine, s.copy_w.at[g]).wait()
-        half = weights.at[g, :, pl.ds(0, outer * part), :]
-        rcopy(half, half, s.pair_ws.at[g], s.pair_wr.at[g], mate).wait_recv()
+        if not four:
+            block = shard_of(g, o, 1 - i)
+            rcopy(block, block, s.pair_ws.at[g], s.pair_wo.at[g], mate).wait_recv()
+        if four:
+            half = weights.at[g, pl.ds(0, 2), pl.ds(0, part), :]
+            rcopy(half, half, s.near_ws.at[g], s.near_wr.at[g], mate).wait_recv()
+        halves = 5 if four else 2 * (outer - 1)
+        both = half_shards(g, halves)
+        rcopy(both, both, s.pair_ws.at[g], s.pair_wr.at[g], mate).wait_recv()
+
+    def half_shards(g, count):
+        return weights.at[g, pl.ds(0, 2), pl.ds(0, count * part), :]
 
     def gather_end(g):
-        half = weights.at[g, :, pl.ds(0, outer * part), :]
-        rcopy(half, half, s.pair_ws.at[g], s.pair_wr.at[g], mate).wait_send()
-        rest = weights.at[g, :, pl.ds(0, (outer - 1) * part), :]
-        rcopy(rest, rest, s.line_ws.at[g], s.line_wr.at[g, 0], mate).wait_send()
+        def sent(sem, halves):
+            both = half_shards(g, halves)
+            rcopy(both, both, sem.at[g], s.pair_wr.at[g], mate).wait_send()
+
+        if not four:
+            sent(s.pair_ws, nd - 2)
+            sent(s.line_ws, nd - 2)
+            rest = shard_of(g, o, i)
+            rcopy(rest, rest, s.own_ws.at[g], s.pair_wr.at[g], mate).wait_send()
+            return
+        sent(s.own_ws, 2)
+        sent(s.pair_ws, 5)
+        sent(s.near_ws, 1)
+
+        @pl.when(middle)
+        def _():
+            sent(s.line_ws, 6)
+            sent(s.far_ws, 2)
+
+        @pl.when(jnp.logical_not(middle))
+        def _():
+            sent(s.line_ws, 4)
 
     def spread_start(k):
         block = gathered.at[k, f]
@@ -295,8 +383,8 @@
         for slot in range(2):
             pair = (1 - y) if slot == 0 else y
 
-            def tile(t, slot=slot, pair=pair):
-                cols = pl.ds(pl.multiple_of(t * hidden, hidden), hidden)
+            for t in range(width // hidden):
+                cols = slice(t * hidden, (t + 1) * hidden)
                 total = None
                 for b_ref, g, j in terms:
                     value = nt(
@@ -304,8 +392,6 @@
                     )
                     total = value if total is None else total + value
                 s.part_sum[slot, :, :, cols] = total.reshape(2, rows, hidden)
-
-            loop(0, width // hidden, tile)
             s.sib_out[par, slot] = s.part_sum[slot, 1 - c].astype(B16)
             rcopy(
                 s.sib_out.at[par, slot],
@@ -408,7 +494,7 @@
         def step(j):
             dst[j, pl.ds(pair * 2, 2)] = as_flat(nn(pair_rows(k, pair), weights[g, j]).astype(B16))
 
-        loop(0, 3, step)
+        each(0, 3, step)
 
     def attend(block):
         spatial = block == 0
@@ -436,10 +522,10 @@
 
     def each_pair(block, step):
         def go(k):
-            lanes = pl.ds(pl.multiple_of((k % n_pairs) * 2 * HDIM, 2 * HDIM), 2 * HDIM)
-            step(k, k // n_pairs, lanes)
-
-        loop(0, (frames if block == 0 else nf) * n_pairs, go)
+            first = (k % n_pairs) * 2 * HDIM
+            step(k, k // n_pairs, slice(first, first + 2 * HDIM))
+
+        each(0, (frames if block == 0 else nf) * n_pairs, go)
 
     def attention(block):
         n, load, store, probs = attend(block)
@@ -516,6 +602,12 @@
             mate,
         ).start()
 
+    def slot_sum(slot):
+        g, j = slot // 4, slot % 4
+        if g < 2:
+            return gin.at[g * 3 + j] if j < 3 else gout.at[g]
+        return gin.at[6 + j] if g == 2 else gout.at[2 + j]
+
     def slot_pass(slot):
         block = s.pair_in.at[slot]
         cp = rcopy(block, block, s.pair_gs.at[slot], s.pair_gr.at[slot], mate)
@@ -537,14 +629,14 @@
             ).start()
 
         each(1, outer, go)
-        gout[slot] = both(o)
+        slot_sum(slot)[...] = both(o)
 
     def slot_end(slot):
         block = s.line_in.at[slot, pl.ds(1, outer - 1)]
         cp = rcopy(block, block, s.line_gs.at[slot], s.line_gr.at[slot], mate)
         cp.wait_recv()
         cp.wait_send()
-        total = gout[slot]
+        total = slot_sum(slot)[...]
         if outer <= 8:
             for q in range(1, outer):
                 total = total + s.line_in[slot, q].astype(F32)
@@ -552,7 +644,7 @@
             total = lax.fori_loop(
                 1, outer, lambda q, t: t + s.line_in[slot, q].astype(F32), total
             )
-        gout[slot] = total
+        slot_sum(slot)[...] = total
         folded = jnp.sum((total * total).reshape(part // 8, 8, hidden), axis=0)
         for k in range(hidden // LANES):
             s.sq_mine[0] += folded[:, k * LANES : (k + 1) * LANES]
@@ -571,7 +663,7 @@
     s.sq_mine[...] = jnp.zeros_like(s.sq_mine)
 
     def masked_rows(block):
-        return jnp.broadcast_to(msk[block, :], (CHUNK, width)) > 0.5
+        return jnp.broadcast_to(s.masked[block, 0:1], (CHUNK, width)) > 0.5
 
     def first_norm(block, k):
         value = jnp.where(masked_rows(block), gains[3:4, :], tok[block, :].astype(F32))
@@ -582,6 +674,7 @@
     spread_start(0)
     round_group(1)
     gather_line(1, 1, outer)
+    gather_own(1)
     gather_pass(0, 1, 2)
 
     def widen(block, k):
@@ -595,9 +688,7 @@
     spread_near(0)
     spread_pass(0)
     gather_pass(0, outer - 1, outer)
-    gather_own(1)
     round_group(2)
-    gather_line(2, 1, 2)
     gather_ready(0)
     project(0, 0, s.qkv.at[0], y)
     spread_far(0)
@@ -616,15 +707,14 @@
     chunks(take_branch)
     pack(1, work)
     swap_start(1)
-    gather_line(2, 2, outer)
+    gather_line(2, 1, outer)
     gather_line(3, 1, outer)
     gather_own(2)
+    gather_own(3)
 
     swap_wait(0)
     gathered[1, f] = swap_in[0].reshape(rows, width)
     spread_start(1)
-    gather_pass(2, 1, 2)
-    gather_own(3)
     swap_wait(1)
 
     def second_norm(block, k):
@@ -639,10 +729,11 @@
     gather_ready(1)
     spread_near(2)
     project(2, 1, s.qkv.at[1], y)
+    gather_pass(2, 1, 2)
     spread_pass(2)
+    gather_pass(2, 2, outer - 1)
     spread_far(2)
     project(2, 1, s.qkv.at[1], 1 - y)
-    gather_pass(2, 2, outer - 1)
     attention(1)
     gather_pass(2, outer - 1, outer)
     collect_start(1, [(s.mixed.at[1], 1, 3)])
@@ -669,7 +760,7 @@
             bend = GELU_A * (1.0 + 3.0 * GELU_B * u * u)
             s.slope[n, pl.ds(pair * 2, 2)] = as_flat(half + 0.5 * u * (1.0 - t * t) * bend)
 
-        loop(0, 4, step)
+        each(0, 4, step)
 
     def down(pair):
         def step(n):
@@ -677,7 +768,7 @@
             slope = s.slope[n, pl.ds(pair * 2, 2)].reshape(2 * rows, hidden)
             s.grad_pre[n, pl.ds(pair * 2, 2)] = as_flat((grad * slope).astype(B16))
 
-        loop(0, 4, step)
+        each(0, 4, step)
 
     gather_ready(2)
     spread_near(3)
@@ -686,7 +777,7 @@
     gather_pass(3, outer - 1, outer)
     spread_far(3)
     up(1 - y)
-    loop(0, 4, lambda n: slot_make(12 + n, 1, s.act.at[n]))
+    each(0, 4, lambda n: slot_make(12 + n, 1, s.act.at[n]))
     slot_send(12)
     slot_send(13)
     gather_ready(3)
@@ -697,7 +788,7 @@
     slot_send(8)
     collect_start(2, [(s.grad_pre.at[n], 2, n) for n in range(4)])
     slot_pass(12)
-    loop(1, 4, lambda n: slot_make(8 + n, 3, s.grad_pre.at[n]))
+    each(1, 4, lambda n: slot_make(8 + n, 3, s.grad_pre.at[n]))
     slot_send(9)
     slot_send(14)
     slot_pass(13)
@@ -732,7 +823,7 @@
     slot_pass(10)
     collect_start(4, [(s.grad_qkv.at[j], 1, j) for j in range(3)])
     slot_pass(15)
-    loop(0, 3, lambda j: slot_make(4 + j, 2, s.grad_qkv.at[j]))
+    each(0, 3, lambda j: slot_make(4 + j, 2, s.grad_qkv.at[j]))
     slot_pass(11)
     get = collect_end(4)
 
@@ -791,19 +882,19 @@
         out[block, :] = mid[block, :].astype(B16)
 
     chunks(give_output)
-    loop(8, 16, slot_end)
+    each(8, 16, slot_end)
     slot_pass(1)
     hear(1, s.vec_in, DP)
     s.vec_mine[...] = total_of(s.vec_in, nd)
     tell(2, lambda to: s.vec_mine, s.vec_side, TP)
     s.vec_side[f] = s.vec_mine[...]
-    loop(4, 8, slot_end)
+    each(4, 8, slot_end)
     slot_end(3)
     slot_pass(2)
     hear(2, s.vec_side, TP)
     grad_vec = total_of(s.vec_side, nf)
     gvec[...] = grad_vec
-    loop(0, 3, slot_end)
+    each(0, 3, slot_end)
 
     lane = lax.broadcasted_iota(jnp.int32, (8, LANES), 1)
     first_lane = (d * part) % LANES
@@ -829,19 +920,10 @@
 def adamw_step(weight, first, second, grad, rate):
     first = BETA_FIRST * first + (1.0 - BETA_FIRST) * grad
     second = BETA_SECOND * second + (1.0 - BETA_SECOND) * grad * grad
-    fix_first = 1.0 - BETA_FIRST**STEP
-    fix_second = 1.0 - BETA_SECOND**STEP
-    update = first / fix_first / (jnp.sqrt(second / fix_second) + ADAM_EPS)
-    return (weight - rate * (update + DECAY_RATE * weight), first, second)
-
-
-def in_slot(j):
-    return jnp.where(j < 3, j, jnp.where(j < 6, j + 1, j + 2))
-
-
-def out_slot(j):
-    k = jnp.minimum(j, 5)
-    return jnp.where(k == 0, 3, jnp.where(k == 1, 7, k + 10))
+    fix_first = 1.0 / (1.0 - BETA_FIRST**STEP)
+    fix_second = 1.0 / (1.0 - BETA_SECOND**STEP)
+    update = (rate * fix_first) * first / (jnp.sqrt(second * fix_second) + ADAM_EPS)
+    return (weight * (1.0 - rate * DECAY_RATE) - update, first, second)
 
 
 def updates(*refs):
@@ -860,11 +942,9 @@
 
     update(0, grad_in[...], RATE_INPUT)
 
-    @pl.when(j < 6)
-    def _():
-        update(1, grad_out[0].T[None], RATE_OUTPUT)
-
-    @pl.when(j == 9)
+    update(1, jnp.stack([grad_out[n].T for n in range(3)]), RATE_OUTPUT)
+
+    @pl.when(j == 1)
     def _():
         update(2, grad_vec[0:4, :], RATE_VECTOR)
         new_out[...] = out[...]
@@ -905,24 +985,25 @@
     vec = as_tile(vectors)
     scratch = scratch_of(z)
     in_vmem = pl.BlockSpec(memory_space=pltpu.VMEM)
-    output, token_grad, norm, grads, grad_vec = pl.pallas_call(
+    output, token_grad, norm, grad_in, grad_out, grad_vec = pl.pallas_call(
         functools.partial(layer, z, list(scratch)),
         out_shape=(
             jax.ShapeDtypeStruct((rows, width), B16),
             jax.ShapeDtypeStruct((rows, width), B16),
             jax.ShapeDtypeStruct((8, LANES), F32),
-            jax.ShapeDtypeStruct((16, part, hidden), F32),
+            jax.ShapeDtypeStruct((10, part, hidden), F32),
+            jax.ShapeDtypeStruct((6, part, hidden), F32),
             jax.ShapeDtypeStruct((8, LANES), F32),
         ),
         in_specs=[in_vmem] * 3 + [pl.BlockSpec(memory_space=pl.ANY)] * 2 + [in_vmem],
-        out_specs=[in_vmem] * 5,
+        out_specs=[in_vmem] * 6,
         scratch_shapes=list(scratch.values()),
         compiler_params=pltpu.CompilerParams(
             collective_id=0, has_side_effects=True, vmem_limit_bytes=VMEM_BYTES
         ),
     )(
         tokens.reshape(rows, width),
-        masks.reshape(rows, 1).astype(F32),
+        masks,
         cotangent.reshape(rows, width),
         by_slot(w_in),
         w_out,
@@ -932,8 +1013,8 @@
     def whole(shape):
         return pl.BlockSpec(shape, lambda j: (0,) * len(shape))
 
-    slot_in = pl.BlockSpec((1, part, hidden), lambda j: (j, 0, 0))
-    slot_out = pl.BlockSpec((1, hidden, part), lambda j: (jnp.minimum(j, 5), 0, 0))
+    slot_in = pl.BlockSpec((5, part, hidden), lambda j: (j, 0, 0))
+    slot_out = pl.BlockSpec((3, hidden, part), lambda j: (j, 0, 0))
     state_specs = [slot_in] * 3 + [slot_out] * 3 + [whole((4, LANES))] * 3
     row_specs = [whole((rows, width))] * 2
     state = (
@@ -949,20 +1030,20 @@
     )
     new = pl.pallas_call(
         updates,
-        grid=(10,),
+        grid=(2,),
         out_shape=tuple(jax.ShapeDtypeStruct(a.shape, F32) for a in state)
         + (jax.ShapeDtypeStruct((rows, width), B16),) * 2
         + (jax.ShapeDtypeStruct((1, 1), F32),),
         in_specs=[
-            pl.BlockSpec((1, part, hidden), lambda j: (in_slot(j), 0, 0)),
-            pl.BlockSpec((1, part, hidden), lambda j: (out_slot(j), 0, 0)),
+            slot_in,
+            pl.BlockSpec((3, part, hidden), lambda j: (j, 0, 0)),
             whole((8, LANES)),
             whole((8, LANES)),
         ]
         + row_specs
         + state_specs,
         out_specs=state_specs + row_specs + [whole((1, 1))],
-    )(grads, grads, grad_vec, norm, output, token_grad, *state)
+    )(grad_in, grad_out, grad_vec, norm, output, token_grad, *state)
     new_w_in, new_m_in, new_v_in, new_w_out, new_m_out, new_v_out = new[:6]
     new_vectors, new_m_vec, new_v_vec, output, token_grad, norm = new[6:]
     return (

time: 273 us -> 249 us (0.912)
  Pallas kernels: 271 us -> 248 us
    pallas_call x1, Pallas kernels: 260 us -> 240 us  [local(): pl.pallas_call(functools.partial(layer, z, list(scratch)), out_shape=(jax...]
    pallas_call x1, Pallas kernels: 11.2 us -> 7.42 us  [local(): pl.pallas_call(updates, grid=(2,), out_shape=tuple((jax.ShapeDtypeStruct(...]
where the time goes in v3:
time: 249 us
  Pallas kernels  248 us (100%)
    pallas_call x1, Pallas kernels, local(): pl.pallas_call(functools.partial(layer, z, list(scratch)), out_shape=(jax...  240 us
    pallas_call x1, Pallas kernels, local(): pl.pallas_call(updates, grid=(2,), out_shape=tuple((jax.ShapeDtypeStruct(...  7.42 us

profile of v3, /device:TPU:0, one launch (start us, length us, event | category | flops | bytes accessed | tf_op | source)
XLA Modules:
  0.0 248.5 jit_solution(1951869981684383884)
XLA Ops:
  0.6 240.3 %shard_map.211 = (bf16[128,1024]{1,0:T(8,128)(2,1)}, bf16[128,1024]{1,0:T(8,128)(2,1)}, f32[8,128]{1,0:T(8,128)}, f32[10,128,256]{2,1,0:T(8,128)}, f32[6,128,256]{2,1,0:T(8,128)}, /*index=5*/f32[8,128]{1,0:T(8,128)}) custom-call(bf16[128,1024]{1,0:T(8,128)(2,1)} %bitcast.15, s32[2,64]{1,0:T(2,128)} %refs_1_.1, bf16[128,1024]{1,0:T(8,128)(2,1)} %bitcast.16, ...), custom_call_target="tpu_custom_call" | custom-call | tf_op jit(solution)/shard_map/pallas_call | solution.py:988
  240.9 7.4 %shard_map.212 = (f32[10,128,256]{2,1,0:T(8,128)}, f32[10,128,256]{2,1,0:T(8,128)}, f32[10,128,256]{2,1,0:T(8,128)}, f32[6,256,128]{2,1,0:T(8,128)}, f32[6,256,1...) custom-call(f32[10,128,256]{2,1,0:T(8,128)} %get-tuple-element.30.re, ...), custom_call_target="tpu_custom_call" | custom-call | tf_op jit(solution)/shard_map/pallas_call | solution.py:1031

commit v4 on v3

--- a/solution.py
+++ b/solution.py
@@ -130,10 +130,10 @@
         near_wr=dma((4,)),
         far_ws=dma((4,)),
         copy_w=dma((4,)),
-        row_s=dma((6, 3)),
-        row_r=dma((6, 3)),
-        sum_s=dma((6, 3)),
-        sum_r=dma((6, 3)),
+        row_s=dma((6, 5)),
+        row_r=dma((6, 5)),
+        sum_s=dma((6, 5)),
+        sum_r=dma((6, 5)),
         swap_s=dma((4,)),
         swap_r=dma((4,)),
         stage_s=dma((16,)),
@@ -217,6 +217,7 @@
         pl.semaphore_signal(bar, inc=1, device_id=dev, device_id_type=MESH)
     pl.semaphore_wait(bar, nd - 1 + nf - 1)
 
+
     def tell(n, src_of, dst, axis):
         count, me = (nd, d) if axis == DP else (nf, f)
 
@@ -355,74 +356,108 @@
         def _():
             sent(s.line_ws, 4)
 
-    def spread_start(k):
-        block = gathered.at[k, f]
-        rcopy(block, block, s.row_s.at[k, 1], s.row_r.at[k, 1], far).start()
-        rcopy(block, block, s.row_s.at[k, 0], s.row_r.at[k, 0], sib).start()
+    def half_rows(h):
+        return pl.ds(h * here, here)
+
+
+    def spread_start(k, h):
+        half = gathered.at[k, f, half_rows(h)]
+        rcopy(half, half, s.row_s.at[k, 1 + h], s.row_r.at[k, 1 + h], far).start()
+        if h == 1:
+            block = gathered.at[k, f]
+            rcopy(block, block, s.row_s.at[k, 0], s.row_r.at[k, 0], sib).start()
 
     def spread_near(k):
         block = gathered.at[k, f_sib]
         rcopy(block, block, s.row_s.at[k, 0], s.row_r.at[k, 0], sib).wait_recv()
 
     def spread_pass(k):
-        block = gathered.at[k, f_far]
-        rcopy(block, block, s.row_s.at[k, 1], s.row_r.at[k, 1], far).wait_recv()
-        rcopy(block, block, s.row_s.at[k, 2], s.row_r.at[k, 2], sib).start()
+        for h in range(2):
+            half = gathered.at[k, f_far, half_rows(h)]
+            rcopy(half, half, s.row_s.at[k, 1 + h], s.row_r.at[k, 1 + h], far).wait_recv()
+            rcopy(half, half, s.row_s.at[k, 3 + h], s.row_r.at[k, 3 + h], sib).start()
 
     def spread_far(k):
-        block = gathered.at[k, f_last]
-        rcopy(block, block, s.row_s.at[k, 2], s.row_r.at[k, 2], sib).wait_recv()
+        for h in range(2):
+            half = gathered.at[k, f_last, half_rows(h)]
+            rcopy(half, half, s.row_s.at[k, 3 + h], s.row_r.at[k, 3 + h], sib).wait_recv()
 
     def spread_end(k):
         block = gathered.at[k, f]
-        for n in range(3):
-            rcopy(block, block, s.row_s.at[k, n], s.row_r.at[k, n], sib).wait_send()
+        rcopy(block, block, s.row_s.at[k, 0], s.row_r.at[k, 0], sib).wait_send()
+        half = gathered.at[k, f, half_rows(0)]
+        for n in range(1, 5):
+            rcopy(half, half, s.row_s.at[k, n], s.row_r.at[k, n], sib).wait_send()
+
+
+    def partial(terms, pick, slot, part_rows):
+        for t in range(width // hidden):
+            cols = slice(t * hidden, (t + 1) * hidden)
+            total = None
+            for b_ref, g, j in terms:
+                b = pick(b_ref)
+                value = nt(b, weights[g, j, cols, :])
+                total = value if total is None else total + value
+            s.part_sum[slot, :, part_rows, cols] = total.reshape(2, -1, hidden)
 
     def collect_start(k, terms):
         par = k % 2
-        for slot in range(2):
-            pair = (1 - y) if slot == 0 else y
-
-            for t in range(width // hidden):
-                cols = slice(t * hidden, (t + 1) * hidden)
-                total = None
-                for b_ref, g, j in terms:
-                    value = nt(
-                        b_ref[pl.ds(pair * 2, 2)].reshape(2 * rows, hidden), weights[g, j, cols, :]
-                    )
-                    total = value if total is None else total + value
-                s.part_sum[slot, :, :, cols] = total.reshape(2, rows, hidden)
-            s.sib_out[par, slot] = s.part_sum[slot, 1 - c].astype(B16)
+
+        def to_sib(slot, part_rows, n):
+            s.sib_out[par, slot, part_rows] = s.part_sum[slot, 1 - c, part_rows].astype(B16)
             rcopy(
-                s.sib_out.at[par, slot],
-                s.sib_in.at[par, slot],
-                s.sum_s.at[k, slot],
-                s.sum_r.at[k, slot],
+                s.sib_out.at[par, slot, part_rows],
+                s.sib_in.at[par, slot, part_rows],
+                s.sum_s.at[k, n],
+                s.sum_r.at[k, n],
                 sib,
             ).start()
-        back = s.sib_in.at[par, 0]
-        rcopy(back, back, s.sum_s.at[k, 0], s.sum_r.at[k, 0], sib).wait_recv()
-        s.far_out[par] = (s.part_sum[0, c] + s.sib_in[par, 0].astype(F32)).astype(B16)
-        rcopy(
-            s.far_out.at[par], s.far_in.at[par], s.sum_s.at[k, 2], s.sum_r.at[k, 2], far
-        ).start()
-
-    def collect_end(k):
+
+        for h in range(2):
+
+            def remote(ref, h=h):
+                return ref[pl.ds((1 - y) * 2, 2), h].reshape(2 * here, hidden)
+
+            partial(terms, remote, 0, half_rows(h))
+            to_sib(0, half_rows(h), h)
+        for h in range(2):
+            half = half_rows(h)
+            back = s.sib_in.at[par, 0, half]
+            rcopy(back, back, s.sum_s.at[k, h], s.sum_r.at[k, h], sib).wait_recv()
+            total = s.part_sum[0, c, half] + s.sib_in[par, 0, half].astype(F32)
+            s.far_out[par, half] = total.astype(B16)
+            rcopy(
+                s.far_out.at[par, half],
+                s.far_in.at[par, half],
+                s.sum_s.at[k, 3 + h],
+                s.sum_r.at[k, 3 + h],
+                far,
+            ).start()
+        partial(
+            terms, lambda ref: ref[pl.ds(y * 2, 2)].reshape(2 * rows, hidden), 1, pl.ds(0, rows)
+        )
+        to_sib(1, pl.ds(0, rows), 2)
+
+    def collect_end(k, h):
         par = k % 2
-        near, away = s.sib_in.at[par, 1], s.far_in.at[par]
-        rcopy(near, near, s.sum_s.at[k, 1], s.sum_r.at[k, 1], sib).wait_recv()
-        rcopy(away, away, s.sum_s.at[k, 2], s.sum_r.at[k, 2], far).wait_recv()
-        for n in range(3):
-            rcopy(near, near, s.sum_s.at[k, n], s.sum_r.at[k, n], sib).wait_send()
-
-        def get(block):
-            return (
-                s.part_sum[1, c, block]
-                + s.sib_in[par, 1, block].astype(F32)
-                + s.far_in[par, block].astype(F32)
-            )
-
-        return get
+        half = half_rows(h)
+        if h == 0:
+            near = s.sib_in.at[par, 1]
+            rcopy(near, near, s.sum_s.at[k, 2], s.sum_r.at[k, 2], sib).wait_recv()
+            rcopy(near, near, s.sum_s.at[k, 2], s.sum_r.at[k, 2], sib).wait_send()
+        away = s.far_in.at[par, half]
+        rcopy(away, away, s.sum_s.at[k, 3 + h], s.sum_r.at[k, 3 + h], far).wait_recv()
+        for n in (h, 3 + h):
+            rcopy(away, away, s.sum_s.at[k, n], s.sum_r.at[k, n], sib).wait_send()
+
+    def collected(k, block):
+        par = k % 2
+        return (
+            s.part_sum[1, c, block]
+            + s.sib_in[par, 1, block].astype(F32)
+            + s.far_in[par, block].astype(F32)
+        )
+
 
     def swap_start(k):
         def go(q):
@@ -464,8 +499,9 @@
 
         loop(0, span, step)
 
-    def chunks(step):
-        loop(0, rows // CHUNK, lambda k: step(pl.ds(pl.multiple_of(k * CHUNK, CHUNK), CHUNK), k))
+    def chunks(step, h):
+        first = h * here // CHUNK
+        each(first, first + here // CHUNK, lambda k: step(pl.ds(k * CHUNK, CHUNK), k))
 
     def norm_rows(n, value, block):
         centered = value - jnp.mean(value, axis=-1, keepdims=True)
@@ -483,6 +519,7 @@
         second = jnp.mean(grad_hat * hat, axis=-1, keepdims=True)
         s.vec_acc[n : n + 1, :] += jnp.sum(grad * hat, axis=0, keepdims=True)
         return rstd * (grad_hat - first - hat * second)
+
 
     def pair_rows(k, pair):
         return gathered[k, pl.ds(pair * 2, 2)].reshape(2 * rows, width)
@@ -587,6 +624,7 @@
         spread_far(k)
         half(1 - y)
 
+
     def slot_make(slot, k, b_ref):
         value = tn(gathered[k].reshape(nf * rows, width), b_ref[...].reshape(nf * rows, hidden))
         s.product[...] = value.reshape(outer, 2, part, hidden)
@@ -670,8 +708,9 @@
         work[block, :] = value
         gathered[0, f, block] = norm_rows(0, value, block)
 
-    chunks(first_norm)
-    spread_start(0)
+    for h in range(2):
+        chunks(first_norm, h)
+        spread_start(0, h)
     round_group(1)
     gather_line(1, 1, outer)
     gather_own(1)
@@ -680,7 +719,8 @@
     def widen(block, k):
         s.part_sum[0, 0, block, :] = cot[block, :].astype(F32)
 
-    chunks(widen)
+    for h in range(2):
+        chunks(widen, h)
     pack(0, s.part_sum.at[0, 0])
     swap_start(0)
 
@@ -699,12 +739,13 @@
     collect_start(0, [(s.mixed.at[0], 0, 3)])
     gather_pass(1, outer - 1, outer)
     round_group(3)
-    get = collect_end(0)
 
     def take_branch(block, k):
-        work[block, :] = work[block, :] + get(block)
-
-    chunks(take_branch)
+        work[block, :] = work[block, :] + collected(0, block)
+
+    for h in range(2):
+        collect_end(0, h)
+        chunks(take_branch, h)
     pack(1, work)
     swap_start(1)
     gather_line(2, 1, outer)
@@ -714,7 +755,8 @@
 
     swap_wait(0)
     gathered[1, f] = swap_in[0].reshape(rows, width)
-    spread_start(1)
+    spread_start(1, 0)
+    spread_start(1, 1)
     swap_wait(1)
 
     def second_norm(block, k):
@@ -722,8 +764,9 @@
         mid[block, :] = value
         gathered[2, f, block] = norm_rows(1, value, block)
 
-    chunks(second_norm)
-    spread_start(2)
+    for h in range(2):
+        chunks(second_norm, h)
+        spread_start(2, h)
     spread_near(1)
     spread_pass(1)
     gather_ready(1)
@@ -738,15 +781,16 @@
     gather_pass(2, outer - 1, outer)
     collect_start(1, [(s.mixed.at[1], 1, 3)])
     gather_pass(3, 1, 2)
-    get = collect_end(1)
 
     def third_norm(block, k):
-        value = mid[block, :] + get(block)
+        value = mid[block, :] + collected(1, block)
         mid[block, :] = value
         gathered[3, f, block] = norm_rows(2, value, block)
 
-    chunks(third_norm)
-    spread_start(3)
+    for h in range(2):
+        collect_end(1, h)
+        chunks(third_norm, h)
+        spread_start(3, h)
     spread_far(1)
     gather_pass(3, 2, outer - 1)
 
@@ -791,47 +835,50 @@
     each(1, 4, lambda n: slot_make(8 + n, 3, s.grad_pre.at[n]))
     slot_send(9)
     slot_send(14)
+    slot_send(10)
+    slot_send(15)
+    slot_send(11)
     slot_pass(13)
-    get = collect_end(2)
 
     def third_back(block, k):
-        value = swap_in[0, k].astype(F32) + norm_back(2, get(block), block)
+        value = swap_in[0, k].astype(F32) + norm_back(2, collected(2, block), block)
         work[block, :] = value
         gathered[4, f, block] = value.astype(B16)
 
-    chunks(third_back)
-    spread_start(4)
+    for h in range(2):
+        collect_end(2, h)
+        chunks(third_back, h)
+        spread_start(4, h)
     slot_pass(8)
-    slot_send(10)
-    slot_send(15)
     collect_start(3, [(s.act.at[n], 3, n) for n in range(4)])
     slot_pass(9)
 
     mixed_back(4, 1)
     slot_make(7, 4, s.mixed.at[1])
     slot_pass(14)
-    slot_send(11)
     slot_send(7)
-    get_output = collect_end(3)
 
     def take_output(block, k):
-        swap_out[2, k] = (mid[block, :] + get_output(block)).astype(B16)
-
-    chunks(take_output)
+        swap_out[2, k] = (mid[block, :] + collected(3, block)).astype(B16)
+
+    for h in range(2):
+        collect_end(3, h)
+        chunks(take_output, h)
     swap_start(2)
     attention_back(1)
     slot_pass(10)
     collect_start(4, [(s.grad_qkv.at[j], 1, j) for j in range(3)])
     slot_pass(15)
     each(0, 3, lambda j: slot_make(4 + j, 2, s.grad_qkv.at[j]))
+
+    def second_back(block, k):
+        swap_out[3, k] = (work[block, :] + norm_back(1, collected(4, block), block)).astype(B16)
+
+    for h in range(2):
+        collect_end(4, h)
+        chunks(second_back, h)
+    swap_start(3)
     slot_pass(11)
-    get = collect_end(4)
-
-    def second_back(block, k):
-        swap_out[3, k] = (work[block, :] + norm_back(1, get(block), block)).astype(B16)
-
-    chunks(second_back)
-    swap_start(3)
     slot_send(4)
     slot_send(5)
     slot_send(6)
@@ -842,13 +889,13 @@
     def take_carry(block, k):
         gathered[5, f, block] = work[block, :].astype(B16)
 
-    chunks(take_carry)
-    spread_start(5)
+    for h in range(2):
+        chunks(take_carry, h)
+        spread_start(5, h)
     slot_pass(7)
     mixed_back(5, 0)
     slot_make(3, 5, s.mixed.at[0])
     slot_send(3)
-    slot_pass(4)
     attention_back(0)
 
     def spatial_slot(j):
@@ -856,19 +903,21 @@
         slot_send(j)
 
     loop(0, 3, spatial_slot)
+    slot_pass(4)
     slot_pass(5)
     collect_start(5, [(s.grad_qkv.at[j], 0, j) for j in range(3)])
     slot_pass(6)
     slot_pass(3)
-    get = collect_end(5)
 
     def first_back(block, k):
-        value = work[block, :] + norm_back(0, get(block), block)
+        value = work[block, :] + norm_back(0, collected(5, block), block)
         masked = masked_rows(block)
         tgr[block, :] = jnp.where(masked, 0.0, value).astype(B16)
         s.vec_acc[3:4, :] += jnp.sum(jnp.where(masked, value, 0.0), axis=0, keepdims=True)
 
-    chunks(first_back)
+    for h in range(2):
+        collect_end(5, h)
+        chunks(first_back, h)
 
     for k in range(width // LANES):
         s.vec_out[k] = s.vec_acc[:, k * LANES : (k + 1) * LANES]
@@ -881,7 +930,8 @@
     def give_output(block, k):
         out[block, :] = mid[block, :].astype(B16)
 
-    chunks(give_output)
+    for h in range(2):
+        chunks(give_output, h)
     each(8, 16, slot_end)
     slot_pass(1)
     hear(1, s.vec_in, DP)
@@ -945,6 +995,7 @@
     update(1, jnp.stack([grad_out[n].T for n in range(3)]), RATE_OUTPUT)
 
     @pl.when(j == 1)
+
     def _():
         update(2, grad_vec[0:4, :], RATE_VECTOR)
         new_out[...] = out[...]

time: 249 us -> 247 us (level)
  no operation moved by 1% of the time
where the time goes in v4:
time: 247 us
  Pallas kernels  246 us (100%)
    pallas_call x1, Pallas kernels, local(): pl.pallas_call(functools.partial(layer, z, list(scratch)), out_shape=(jax...  239 us
    pallas_call x1, Pallas kernels, local(): pl.pallas_call(updates, grid=(2,), out_shape=tuple((jax.ShapeDtypeStruct(...  7.42 us

profile of v4, /device:TPU:0, one launch (start us, length us, event | category | flops | bytes accessed | tf_op | source)
XLA Modules:
  0.0 247.1 jit_solution(10806125446385966939)
XLA Ops:
  0.6 238.8 %shard_map.211 = (bf16[128,1024]{1,0:T(8,128)(2,1)}, bf16[128,1024]{1,0:T(8,128)(2,1)}, f32[8,128]{1,0:T(8,128)}, f32[10,128,256]{2,1,0:T(8,128)}, f32[6,128,256]{2,1,0:T(8,128)}, /*index=5*/f32[8,128]{1,0:T(8,128)}) custom-call(bf16[128,1024]{1,0:T(8,128)(2,1)} %bitcast.15, s32[2,64]{1,0:T(2,128)} %refs_1_.1, bf16[128,1024]{1,0:T(8,128)(2,1)} %bitcast.16, ...), custom_call_target="tpu_custom_call" | custom-call | tf_op jit(solution)/shard_map/pallas_call | solution.py:1039
  239.5 7.4 %shard_map.212 = (f32[10,128,256]{2,1,0:T(8,128)}, f32[10,128,256]{2,1,0:T(8,128)}, f32[10,128,256]{2,1,0:T(8,128)}, f32[6,256,128]{2,1,0:T(8,128)}, f32[6,256,1...) custom-call(f32[10,128,256]{2,1,0:T(8,128)} %get-tuple-element.30.re, ...), custom_call_target="tpu_custom_call" | custom-call | tf_op jit(solution)/shard_map/pallas_call | solution.py:1082

commit v5 on v4

--- a/solution.py
+++ b/solution.py
@@ -864,7 +864,6 @@
     for h in range(2):
         collect_end(3, h)
         chunks(take_output, h)
-    swap_start(2)
     attention_back(1)
     slot_pass(10)
     collect_start(4, [(s.grad_qkv.at[j], 1, j) for j in range(3)])
@@ -879,6 +878,7 @@
         chunks(second_back, h)
     swap_start(3)
     slot_pass(11)
+    swap_start(2)
     slot_send(4)
     slot_send(5)
     slot_send(6)
@@ -896,6 +896,7 @@
     mixed_back(5, 0)
     slot_make(3, 5, s.mixed.at[0])
     slot_send(3)
+    slot_pass(4)
     attention_back(0)
 
     def spatial_slot(j):
@@ -903,7 +904,6 @@
         slot_send(j)
 
     loop(0, 3, spatial_slot)
-    slot_pass(4)
     slot_pass(5)
     collect_start(5, [(s.grad_qkv.at[j], 0, j) for j in range(3)])
     slot_pass(6)

time: 247 us -> 243 us (0.984)
  Pallas kernels: 246 us -> 242 us
    pallas_call x1, Pallas kernels: 239 us -> 234 us  [local(): pl.pallas_call(functools.partial(layer, z, list(scratch)), out_shape=(jax...]
where the time goes in v5:
time: 243 us
  Pallas kernels  242 us (100%)
    pallas_call x1, Pallas kernels, local(): pl.pallas_call(functools.partial(layer, z, list(scratch)), out_shape=(jax...  234 us
    pallas_call x1, Pallas kernels, local(): pl.pallas_call(updates, grid=(2,), out_shape=tuple((jax.ShapeDtypeStruct(...  7.42 us

profile of v5, /device:TPU:0, one launch (start us, length us, event | category | flops | bytes accessed | tf_op | source)
XLA Modules:
  0.0 242.7 jit_solution(9504125496720844354)
XLA Ops:
  0.6 234.5 %shard_map.211 = (bf16[128,1024]{1,0:T(8,128)(2,1)}, bf16[128,1024]{1,0:T(8,128)(2,1)}, f32[8,128]{1,0:T(8,128)}, f32[10,128,256]{2,1,0:T(8,128)}, f32[6,128,256]{2,1,0:T(8,128)}, /*index=5*/f32[8,128]{1,0:T(8,128)}) custom-call(bf16[128,1024]{1,0:T(8,128)(2,1)} %bitcast.15, s32[2,64]{1,0:T(2,128)} %refs_1_.1, bf16[128,1024]{1,0:T(8,128)(2,1)} %bitcast.16, ...), custom_call_target="tpu_custom_call" | custom-call | tf_op jit(solution)/shard_map/pallas_call | solution.py:1039
  235.1 7.4 %shard_map.212 = (f32[10,128,256]{2,1,0:T(8,128)}, f32[10,128,256]{2,1,0:T(8,128)}, f32[10,128,256]{2,1,0:T(8,128)}, f32[6,256,128]{2,1,0:T(8,128)}, f32[6,256,1...) custom-call(f32[10,128,256]{2,1,0:T(8,128)} %get-tuple-element.30.re, ...), custom_call_target="tpu_custom_call" | custom-call | tf_op jit(solution)/shard_map/pallas_call | solution.py:1082

commit v6 on v5

--- a/solution.py
+++ b/solution.py
@@ -980,27 +980,49 @@
     grad_in, grad_out, grad_vec, norm, out, tgr = refs[:6]
     state = refs[6:15]
     new = refs[15:24]
-    new_out, new_tgr, new_norm = refs[24:]
-    j = pl.program_id(0)
+    new_out, new_tgr, new_norm = refs[24:27]
+    held = refs[27:35]
+    in_s, out_s = refs[35:]
+    pieces = [(0, 2 * n) for n in range(5)] + [(1, 2 * n) for n in range(3)]
+
+    def load(p, k):
+        kind, first = pieces[p]
+        slots = pl.ds(first, 2)
+        source = state[3 * kind + k] if k < 3 else (grad_out if kind else grad_in)
+        return pltpu.make_async_copy(source.at[slots], held[4 * kind + k].at[slots], in_s.at[p, k])
+
+    def store(p, k):
+        kind, first = pieces[p]
+        slots = pl.ds(first, 2)
+        return pltpu.make_async_copy(
+            held[4 * kind + k].at[slots], new[3 * kind + k].at[slots], out_s.at[p, k]
+        )
+
+    for p in range(len(pieces)):
+        for k in range(4):
+            load(p, k).start()
     grad_norm = norm[0:1, 0:1]
     factor = CLIP_AT / jnp.maximum(grad_norm, CLIP_AT)
-
-    def update(n, grad, rate):
-        values = adamw_step(*(state[3 * n + k][...] for k in range(3)), grad * factor, rate)
+    new_norm[...] = grad_norm
+    new_out[...] = out[...]
+    new_tgr[...] = tgr[...]
+    values = adamw_step(*(state[6 + k][...] for k in range(3)), grad_vec[0:4, :] * factor, RATE_VECTOR)
+    for k in range(3):
+        new[6 + k][...] = values[k]
+    for p, (kind, first) in enumerate(pieces):
+        for k in range(4):
+            load(p, k).wait()
+        for n in range(first, first + 2):
+            weight, one, two, grad = (held[4 * kind + k][n] for k in range(4))
+            grad = (grad.T if kind else grad) * factor
+            values = adamw_step(weight, one, two, grad, RATE_OUTPUT if kind else RATE_INPUT)
+            for k in range(3):
+                held[4 * kind + k][n] = values[k]
         for k in range(3):
-            new[3 * n + k][...] = values[k]
-
-    update(0, grad_in[...], RATE_INPUT)
-
-    update(1, jnp.stack([grad_out[n].T for n in range(3)]), RATE_OUTPUT)
-
-    @pl.when(j == 1)
-
-    def _():
-        update(2, grad_vec[0:4, :], RATE_VECTOR)
-        new_out[...] = out[...]
-        new_tgr[...] = tgr[...]
-        new_norm[...] = grad_norm
+            store(p, k).start()
+    for p in range(len(pieces)):
+        for k in range(3):
+            store(p, k).wait()
 
 
 def local(tokens, masks, cotangent, w_in, w_out, vectors, m_in, m_out, m_vec, v_in, v_out, v_vec):
@@ -1061,13 +1083,7 @@
         vec,
     )
 
-    def whole(shape):
-        return pl.BlockSpec(shape, lambda j: (0,) * len(shape))
-
-    slot_in = pl.BlockSpec((5, part, hidden), lambda j: (j, 0, 0))
-    slot_out = pl.BlockSpec((3, hidden, part), lambda j: (j, 0, 0))
-    state_specs = [slot_in] * 3 + [slot_out] * 3 + [whole((4, LANES))] * 3
-    row_specs = [whole((rows, width))] * 2
+    anywhere = pl.BlockSpec(memory_space=pl.ANY)
     state = (
         by_slot(w_in),
         by_slot(m_in),
@@ -1081,19 +1097,16 @@
     )
     new = pl.pallas_call(
         updates,
-        grid=(2,),
         out_shape=tuple(jax.ShapeDtypeStruct(a.shape, F32) for a in state)
         + (jax.ShapeDtypeStruct((rows, width), B16),) * 2
         + (jax.ShapeDtypeStruct((1, 1), F32),),
-        in_specs=[
-            slot_in,
-            pl.BlockSpec((3, part, hidden), lambda j: (j, 0, 0)),
-            whole((8, LANES)),
-            whole((8, LANES)),
-        ]
-        + row_specs
-        + state_specs,
-        out_specs=state_specs + row_specs + [whole((1, 1))],
+        in_specs=[anywhere] * 2 + [in_vmem] * 4 + [anywhere] * 6 + [in_vmem] * 3,
+        out_specs=[anywhere] * 6 + [in_vmem] * 6,
+        scratch_shapes=[pltpu.VMEM((10, part, hidden), F32)] * 4
+        + [pltpu.VMEM((6, hidden, part), F32)] * 3
+        + [pltpu.VMEM((6, part, hidden), F32)]
+        + [pltpu.SemaphoreType.DMA((8, 4)), pltpu.SemaphoreType.DMA((8, 3))],
+        compiler_params=pltpu.CompilerParams(vmem_limit_bytes=40 << 20),
     )(grad_in, grad_out, grad_vec, norm, output, token_grad, *state)
     new_w_in, new_m_in, new_v_in, new_w_out, new_m_out, new_v_out = new[:6]
     new_vectors, new_m_vec, new_v_vec, output, token_grad, norm = new[6:]

time: 243 us -> 256 us (1.053); the launches traced: 243 us -> 252 us
  local copies, waits for them, and re-layouts: 0 us -> 11.9 us
  Pallas kernels: 242 us -> 239 us
    unnamed x0 -> x30, local copies, waits for them, and re-layouts: none -> 11.9 us
    pallas_call x1, Pallas kernels: 7.42 us -> 4.84 us  [local(): pl.pallas_call(updates, out_shape=tuple((jax.ShapeDtypeStruct(a.shape, F3...]
where the time goes in v6:
time: 256 us; the launch traced here: 252 us
  Pallas kernels  239 us (93%)
  local copies, waits for them, and re-layouts  11.9 us (5%)
    pallas_call x1, Pallas kernels, local(): pl.pallas_call(functools.partial(layer, z, list(scratch)), out_shape=(jax...  234 us
    unnamed x30, local copies, waits for them, and re-layouts  11.9 us

profile of v6, /device:TPU:0, one launch (start us, length us, event | category | flops | bytes accessed | tf_op | source)
XLA Modules:
  0.0 252.5 jit_solution(10564822755422562212)
XLA Ops:
  0.6 0.0 copy-start.1
  0.7 0.0 copy-start.10
  0.7 0.0 copy-start.13
  0.7 0.0 copy-start.14
  0.7 234.5 %shard_map.211 = (bf16[128,1024]{1,0:T(8,128)(2,1)}, bf16[128,1024]{1,0:T(8,128)(2,1)}, f32[8,128]{1,0:T(8,128)}, f32[10,128,256]{2,1,0:T(8,128)}, f32[6,128,256]{2,1,0:T(8,128)}, /*index=5*/f32[8,128]{1,0:T(8,128)}) custom-call(bf16[128,1024]{1,0:T(8,128)(2,1)} %bitcast.15, s32[2,64]{1,0:T(2,128)} %refs_1_.1, bf16[128,1024]{1,0:T(8,128)(2,1)} %bitcast.16, ...), custom_call_target="tpu_custom_call" | custom-call | tf_op jit(solution)/shard_map/pallas_call | solution.py:1061
  235.2 0.0 copy-done.1
  235.2 0.0 copy-done.10
  235.2 0.0 copy-done.13
  235.2 0.0 copy-done.14
  235.2 0.0 copy-start
  235.2 1.3 copy-done
  236.6 0.0 copy-start.2
  236.6 1.3 copy-done.2
  237.9 0.0 copy-start.3
  237.9 1.3 copy-done.3
  239.2 1.3 copy-done.4
  240.5 1.1 copy-done.5
  241.6 1.1 copy-done.6
  242.8 1.1 copy-done.7
  243.9 0.9 copy-done.8
  244.9 0.9 copy-done.9
  245.8 0.7 copy-done.11
  246.5 0.7 copy-done.12
  247.2 4.8 %shard_map.212 = (f32[10,128,256]{2,1,0:T(8,128)}, f32[10,128,256]{2,1,0:T(8,128)}, f32[10,128,256]{2,1,0:T(8,128)}, f32[6,256,128]{2,1,0:T(8,128)}, f32[6,256,1...) custom-call(f32[10,128,256]{2,1,0:T(8,128)S(1)} %copy-done.4, ...), custom_call_target="tpu_custom_call" | custom-call | tf_op jit(solution)/shard_map/pallas_call | solution.py:1098
  (8 shorter events, 0.0 us)
Async XLA Ops:
  0.6 234.5 %copy-start.1 = (f32[6,256,128]{2,1,0:T(8,128)S(1)}, f32[6,256,128]{2,1,0:T(8,128)}, u32[]{:S(2)}) copy-start(f32[6,256,128]{2,1,0:T(8,128)} %refs_9_.1) | copy-start | bytes 2359300
  0.7 234.5 %copy-start.10 = (f32[4,128]{1,0:T(4,128)S(1)}, f32[4,128]{1,0:T(4,128)}, u32[]{:S(2)}) copy-start(f32[4,128]{1,0:T(4,128)} %refs_12_.1) | copy-start | bytes 6148
  0.7 234.5 %copy-start.13 = (f32[4,128]{1,0:T(4,128)S(1)}, f32[4,128]{1,0:T(4,128)}, u32[]{:S(2)}) copy-start(f32[4,128]{1,0:T(4,128)} %refs_13_.1) | copy-start | bytes 6148
  0.7 234.5 %copy-start.14 = (f32[4,128]{1,0:T(4,128)S(1)}, f32[4,128]{1,0:T(4,128)}, u32[]{:S(2)}) copy-start(f32[4,128]{1,0:T(4,128)} %refs_14_.1) | copy-start | bytes 6148
  235.2 1.3 copy-start
  236.6 1.3 copy-start.2
  237.9 1.3 copy-start.3
  239.2 1.3 copy-start.4
  240.5 1.1 copy-start.5
  241.6 1.1 copy-start.6
  242.8 1.1 copy-start.7
  243.9 0.9 copy-start.8
  244.9 0.9 copy-start.9
  245.8 0.7 copy-start.11
  246.5 0.7 copy-start.12
